TPU v7x, 512 devices: a whole 4x8x8 slice. The times are simulated.
512 devices in a mesh: grp: 16 (over x_hi, z), sp: 32 (over y, x_lo, core).
Axes of the slice: x: 4 (x_hi: 2, x_lo: 2; x = x_hi * 2 + x_lo), y: 8, z: 8, core: 2. Of those that a mesh axis runs over, the one named last changes fastest.
Arguments:
- residual_in: bfloat16 [16, 32, 24, 3072], P('grp', 'sp'), may hold values from -36 to 36
- cached: bfloat16 [2, 16, 32, 24, 3072], P(None, 'grp', 'sp'), may hold values from -3 to 3
- use_cached: int32 [2, 16, 32, 24], P(None, 'grp', 'sp'), may hold values 0 or 1
- queries: bfloat16 [16, 32, 24, 2048], P('grp', 'sp'), may hold values from -6.8 to 6.8
- attn_keys: bfloat16 [16, 32, 24, 2048], P('grp', 'sp'), may hold values from -6.8 to 6.8
- values: bfloat16 [16, 32, 24, 2048], P('grp', 'sp'), may hold values from -6 to 6
- gate_mod: float32 [3072], replicated, may hold values from 1 to 4
- shift_mod: float32 [3072], replicated, may hold values from -3 to 3
- scale_mod: float32 [3072], replicated, may hold values from -0.5 to 0.5
- out_weight: bfloat16 [2048, 3072], P('grp'), may hold values from -0.125 to 0.125
- final_weight: bfloat16 [3072, 64], replicated, may hold values from -0.109375 to 0.109375
- final_bias: float32 [64], replicated, may hold values from -2 to 2
- first_weight: bfloat16 [3, 3, 3, 16, 512], replicated, may hold values from -0.3125 to 0.3125
- first_bias: float32 [512], replicated, may hold values from -2 to 2
- second_weight: bfloat16 [512, 3, 3, 3, 512], P('sp'), may hold values from -0.0546875 to 0.0546875
Outputs:
- stream: bfloat16 [16, 32, 24, 3072], P('grp', 'sp')
- decoded: bfloat16 [512, 48, 1024], P('sp', 'grp')
All inputs are finite; a program needn't handle non-finite values. No bound on the sum of `use_cached` on one device may be relied on, other than what follows from the above.
Results may differ from a plain program's by a relative error of at most 0.02.
Values may be sent and summed in bfloat16 or wider, within the bound.
No kernel may reach another device: no remote copies, remote signals or barrier semaphores. Data moves between devices by JAX's collectives and lax.ppermute only.
A program may use at most 128 MiB of HBM per device.

v0:
```python
import math

import jax
import jax.numpy as jnp
from jax import lax
from jax.sharding import PartitionSpec as P

HD = 128
HEADS = 16


neg_large = -1e30
key_block_cap = 2048


def with_halo(block, sides, width):
    for axis, dim in sides:
        count = lax.axis_size(axis)
        forward = [(i, i + 1) for i in range(count - 1)]
        backward = [(target, source) for source, target in forward]
        low = lax.ppermute(
            lax.slice_in_dim(block, block.shape[dim] - width, None, axis=dim), axis, forward
        )
        high = lax.ppermute(lax.slice_in_dim(block, 0, width, axis=dim), axis, backward)
        block = jnp.concatenate([low, block, high], axis=dim)
    return block


def online_update(state_now, query_matrix_rows, key_matrix_rows, value_rows, factor):
    running_max, running_sum, accumulated = state_now
    scores = (
        jnp.einsum(
            "tiv,uiv->itu", query_matrix_rows, key_matrix_rows, preferred_element_type=jnp.float32
        )
        * factor
    )
    new_max = jnp.maximum(running_max, jnp.max(scores, axis=2))
    shrink = jnp.exp(running_max - new_max)
    weights_now = jnp.exp(scores - new_max[:, :, None])
    running_sum = running_sum * shrink + jnp.sum(weights_now, axis=2)
    update = jnp.einsum(
        "api,iak->apk",
        weights_now.astype(jnp.bfloat16),
        value_rows,
        preferred_element_type=jnp.float32,
    )
    accumulated = accumulated * shrink[:, :, None] + update
    return (new_max, running_sum, accumulated)


def attend(exchanged):
    query_four, key_four, value_four = exchanged
    query_all = query_four[:, 0]
    query_count, heads_here, head_width = query_all.shape
    key_all = key_four[:, 0]
    value_all = value_four[:, 0]
    factor = 1.0 / math.sqrt(head_width)
    initial = (
        jnp.full((heads_here, query_count), neg_large, jnp.float32),
        jnp.zeros((heads_here, query_count), jnp.float32),
        jnp.zeros((heads_here, query_count, head_width), jnp.float32),
    )
    key_piece = lax.all_gather(key_all, "sp", axis=0, tiled=True)
    value_piece = lax.all_gather(value_all, "sp", axis=0, tiled=True)
    piece_rows = key_piece.shape[0]
    block_rows = piece_rows
    while block_rows > key_block_cap and block_rows % 2 == 0:
        block_rows = block_rows // 2
    block_count = piece_rows // block_rows
    key_blocks = key_piece.reshape(block_count, block_rows, heads_here, head_width)
    value_blocks = value_piece.reshape(block_count, block_rows, heads_here, head_width)

    def scan_step(state_inner, key_value):
        return (online_update(state_inner, query_all, key_value[0], key_value[1], factor), None)

    state_out, unused = lax.scan(scan_step, initial, (key_blocks, value_blocks))
    running_max, running_sum, accumulated = state_out
    result = accumulated / running_sum[:, :, None]
    return jnp.transpose(result, (1, 0, 2)).astype(jnp.bfloat16)[:, None]


def slice_start(time_tap, row_tap, col_start):
    return (
        jnp.asarray(time_tap, jnp.int32),
        jnp.asarray(row_tap, jnp.int32),
        jnp.asarray(col_start, jnp.int32),
        jnp.asarray(0, jnp.int32),
    )


def first_conv(
    latent_band, first_weight, first_bias, col_first, col_count, band_index, band_rows, lat_height
):
    frame_count = latent_band.shape[0]
    rim_rows = latent_band.shape[1] - 2
    lat_channels = latent_band.shape[3]
    padded = jnp.concatenate([latent_band[:1], latent_band[:1], latent_band], axis=0)
    padded = jnp.pad(padded, ((0, 0), (0, 0), (1, 1), (0, 0)))
    tap_slices = []
    for time_tap in range(3):
        for row_tap in range(3):
            for col_tap in range(3):
                tap_slices.append(
                    lax.dynamic_slice(
                        padded,
                        slice_start(time_tap, row_tap, col_first + col_tap),
                        (frame_count, rim_rows, col_count, lat_channels),
                    )
                )
    patches = jnp.concatenate(tap_slices, axis=3)
    conv_filter = first_weight.reshape(27 * lat_channels, first_weight.shape[4])
    first_out = jnp.dot(patches, conv_filter, preferred_element_type=jnp.float32) + first_bias
    global_rows = band_index * band_rows - 1 + jnp.arange(rim_rows, dtype=jnp.int32)
    inside = (global_rows >= 0) & (global_rows < lat_height)
    first_out = jnp.where(inside[None, :, None, None], first_out, 0.0)
    return first_out.astype(jnp.bfloat16)


def per_device(
    residual_in,
    cached,
    use_cached,
    queries,
    attn_keys,
    values,
    gate_mod,
    shift_mod,
    scale_mod,
    out_weight,
    final_weight,
    final_bias,
    first_weight,
    first_bias,
    second_weight,
):
    frames_here, cols_here, rows_here, model_width = residual_in.shape
    count_of_tokens = frames_here * cols_here * rows_here
    groups = lax.axis_size("grp")
    lanes = lax.axis_size("sp")
    heads_group = HEADS // groups

    def split_heads(array):
        return array.reshape(count_of_tokens, groups, heads_group, HD)

    attended = attend(
        (
            lax.all_to_all(split_heads(queries), "grp", split_axis=1, concat_axis=0, tiled=True),
            lax.all_to_all(split_heads(attn_keys), "grp", split_axis=1, concat_axis=0, tiled=True),
            lax.all_to_all(split_heads(values), "grp", split_axis=1, concat_axis=0, tiled=True),
        )
    )
    flat_attended = attended.reshape(
        groups * count_of_tokens, attended.shape[2] * attended.shape[3]
    )
    projected_output = lax.psum_scatter(
        jnp.dot(flat_attended, out_weight, preferred_element_type=jnp.float32).astype(jnp.bfloat16),
        "grp",
        scatter_dimension=0,
        tiled=True,
    ).astype(jnp.float32)
    mixed = residual_in.reshape(count_of_tokens, model_width).astype(jnp.float32)
    selection = use_cached.reshape(use_cached.shape[0], count_of_tokens).astype(jnp.float32)
    for index_b in range(cached.shape[0]):
        mixed = mixed + selection[index_b][:, None] * cached[index_b].reshape(
            count_of_tokens, model_width
        ).astype(jnp.float32)
    stream_out = (mixed + gate_mod[None, :] * projected_output).astype(jnp.bfloat16)
    normed_in = stream_out.astype(jnp.float32)
    center = jnp.mean(normed_in, axis=1, keepdims=True)
    spread = jnp.mean(jnp.square(normed_in - center), axis=1, keepdims=True)
    modulated = (
        (normed_in - center) * lax.rsqrt(spread + 1e-06) * (1.0 + scale_mod)[None, :]
        + shift_mod[None, :]
    ).astype(jnp.bfloat16)
    latent_tokens = (
        jnp.dot(modulated, final_weight, preferred_element_type=jnp.float32) + final_bias[None, :]
    ).astype(jnp.bfloat16)
    lat_channels = latent_tokens.shape[1] // 4
    split_tokens = latent_tokens.reshape(frames_here, cols_here, rows_here, 2, 2, lat_channels)
    arranged = jnp.transpose(split_tokens, (0, 2, 3, 1, 4, 5)).reshape(
        frames_here, 2 * rows_here, 2 * cols_here * lat_channels
    )
    lat_height = 2 * rows_here
    band_rows = lat_height // groups
    bordered = jnp.pad(arranged, ((0, 0), (2, 2), (0, 0)))
    window_index = (
        jnp.arange(groups, dtype=jnp.int32)[:, None] * band_rows
        + jnp.arange(band_rows + 4, dtype=jnp.int32)[None, :]
    )
    windows = bordered[:, window_index]
    moved = lax.all_to_all(windows, "grp", split_axis=1, concat_axis=0, tiled=True)
    frame_count = groups * frames_here
    band_local = moved.reshape(frame_count, band_rows + 4, 2 * cols_here * lat_channels)
    lat_width = 2 * cols_here * lanes
    band_index = lax.axis_index("grp")
    lane_index = lax.axis_index("sp")
    col_count = 2 * cols_here
    own_band = band_local.reshape(frame_count, band_rows + 4, col_count, lat_channels)
    edged = with_halo(own_band, (("sp", 2),), 1)
    first_part = first_conv(
        edged, first_weight, first_bias, 1, col_count, band_index, band_rows, lat_height
    )
    first_full = lax.all_gather(first_part, "sp", axis=2, tiled=True)
    activated = jax.nn.silu(first_full.astype(jnp.float32)).astype(jnp.bfloat16)
    act_pad = jnp.concatenate([activated[:1], activated[:1], activated], axis=0)
    act_pad = jnp.pad(act_pad, ((0, 0), (0, 0), (1, 1), (0, 0)))
    own_channels = second_weight.shape[0]
    summed_total = lax.conv_general_dilated(
        act_pad[None],
        second_weight,
        (1, 1, 1),
        "VALID",
        dimension_numbers=("NDHWC", "ODHWI", "NDHWC"),
        preferred_element_type=jnp.float32,
    )[0]
    residual_part = lax.dynamic_slice_in_dim(
        first_full[:, 1 : band_rows + 1], lane_index * own_channels, own_channels, 3
    )
    cells_out = (summed_total + residual_part.astype(jnp.float32)).astype(jnp.bfloat16)
    decoded = jnp.transpose(cells_out, (3, 1, 0, 2)).reshape(
        own_channels, band_rows, frame_count * lat_width
    )
    return (stream_out.reshape(residual_in.shape), decoded)


def solution(mesh):
    return jax.shard_map(
        per_device,
        mesh=mesh,
        in_specs=(
            P("grp", "sp", None, None),
            P(None, "grp", "sp", None, None),
            P(None, "grp", "sp", None),
            P("grp", "sp", None, None),
            P("grp", "sp", None, None),
            P("grp", "sp", None, None),
            P(),
            P(),
            P(),
            P("grp", None),
            P(),
            P(),
            P(),
            P(),
            P("sp", None, None, None, None),
        ),
        out_specs=(P("grp", "sp", None, None), P("sp", "grp", None)),
        check_vma=False,
    )
```

profile of v0, /device:TPU:1, one launch (start us, length us, event | category | flops | bytes accessed | tf_op | source)
XLA Modules:
  0.0 575.2 jit_solution(1601950850541055950)
XLA Ops:
  7.2 1.0 copy.97
  8.2 22.3 %all_to_all.54 = bf16[24,16,1,128]{3,0,2,1:T(8,128)(2,1)} all-to-all(bf16[24,16,1,128]{3,0,2,1:T(8,128)(2,1)S(1)} %copy.75), channel_id=1, replica_groups=mesh['grp'=16,'sp'=32] {'grp'}, dimensions={1} | all-to-all | bytes 196608 | tf_op jit(solution)/shard_map/all_to_all | solution.py:148
  30.6 0.9 copy.99
  31.6 12.3 %all_to_all.55 = bf16[24,16,1,128]{3,0,2,1:T(8,128)(2,1)} all-to-all(bf16[24,16,1,128]{3,0,2,1:T(8,128)(2,1)S(1)} %copy.77), channel_id=1, replica_groups=mesh['grp'=16,'sp'=32] {'grp'}, dimensions={1} | all-to-all | bytes 196608 | tf_op jit(solution)/shard_map/all_to_all | solution.py:149
  43.9 0.9 copy.98
  44.8 0.7 copy.76
  45.5 3.5 all-to-all-start.1
  49.1 8.9 %all-to-all-done.1 = bf16[24,16,1,128]{3,0,2,1:T(8,128)(2,1)S(1)} async-done(((bf16[24,16,1,128]{3,0,2,1:T(8,128)(2,1)}), bf16[24,16,1,128]{3,0,2,1:T(8,128)(2,1)S(1)}, u32[]{:S(2)}, u32[]{:S(2)}) %all-to-all-start.1) | async-done | bytes 98336 | tf_op jit(solution)/shard_map/all_to_all | solution.py:147
  57.9 37.9 %all-gather.4.cloned.1.call-done = bf16[12288,1,128]{2,0,1:T(8,128)(2,1)} async-done(((bf16[384,1,128]{2,0,1:T(8,128)(2,1)}), bf16[12288,1,128]{2,0,1:T(8,128)(2,1)}) %all-gather.4.cloned.1.call-update) | async-done | bytes 3145744 | tf_op jit(solution)/shard_map/all_gather | solution.py:63
  95.8 70.4 %all-gather.6.cloned.1.call-done = bf16[12288,1,128]{2,0,1:T(8,128)(2,1)} async-done(((bf16[384,1,128]{2,0,1:T(8,128)(2,1)}), bf16[12288,1,128]{2,0,1:T(8,128)(2,1)}) %all-gather.6.cloned.1.call-update) | async-done | bytes 3145744 | tf_op jit(solution)/shard_map/all_gather | solution.py:64
  166.2 28.4 %while.15 = (s32[]{:T(128)}, f32[1,384]{1,0:T(1,128)S(1)}, f32[1,384]{1,0:T(1,128)S(1)}, f32[1,384,128]{2,1,0:T(8,128)S(1)}, bf16[8,1536,1,128]{3,1,2,0:T(8,128)...) while((s32[]{:T(128)}, f32[1,384]{1,0:T(1,128)S(1)}, ...), condition=%wide.region_3.4_spmd.clone, body=%wide.region_0.3_spmd.clone.sunk | while | flops 305678592 | bytes 8382073 | solution.py:76
  166.2 1.5 fusion.98
  167.7 0.4 fusion.100
  168.1 1.6 fusion.102
  169.7 1.5 fusion.98
  171.2 0.4 fusion.100
  171.6 1.6 fusion.102
  173.3 1.5 fusion.98
  174.8 0.4 fusion.100
  175.2 1.6 fusion.102
  176.8 1.5 fusion.98
  178.3 0.4 fusion.100
  178.7 1.6 fusion.102
  180.4 1.5 fusion.98
  181.9 0.4 fusion.100
  182.3 1.6 fusion.102
  183.9 1.5 fusion.98
  185.5 0.4 fusion.100
  185.9 1.6 fusion.102
  187.5 1.5 fusion.98
  189.0 0.4 fusion.100
  189.4 1.6 fusion.102
  191.1 1.5 fusion.98
  192.6 0.4 fusion.100
  193.0 1.6 fusion.102
  194.7 2.3 convolution_convert_fusion
  197.3 212.3 %reduce-scatter.2.cloned.1.call-done = bf16[24,3072]{1,0:T(8,128)(2,1)} async-done(((bf16[384,3072]{1,0:T(8,128)(2,1)}), bf16[24,3072]{1,0:T(8,128)(2,1)}) %reduce-scatter.2.cloned.1.call-update) | async-done | bytes 147472 | tf_op jit(solution)/shard_map/reduce_scatter | solution.py:155
  409.6 1.2 convert_reduce_fusion
  410.8 0.2 fusion.52
  411.1 0.3 fusion.48
  411.5 0.7 gather_fusion
  412.2 0.6 reshape.179
  412.8 5.0 all-to-all-start.3
  417.9 8.8 %all-to-all-done.3 = bf16[1,16,7,32]{3,2,0,1:T(8,128)(2,1)S(1)} async-done(((bf16[1,16,7,32]{3,2,0,1:T(8,128)(2,1)}), bf16[1,16,7,32]{3,2,0,1:T(8,128)(2,1)S(1)}, u32[]{:S(2)}, u32[]{:S(2)}) %all-to-all-start.3) | async-done | bytes 7200 | tf_op jit(solution)/shard_map/all_to_all | solution.py:191
  426.9 9.6 %collective-permute-start = (bf16[16,7,1,16]{3,0,2,1:T(8,128)(2,1)S(1)}, bf16[16,7,1,16]{3,0,2,1:T(8,128)(2,1)S(1)}, u32[]{:S(2)}, u32[]{:S(2)}) collective-permute-start(bf16[16,7,1,16]{3,0,2,1:T(8,128)(2,1)S(1)} %copy.103), channel_id=1, source_target_pairs={{0,1},{1,2},{2,3},{3,4},{4,5},{5,6},{6,7},{7,8},{8,9},{9,10},{10,1... | collective-permute-start | bytes 10760 | tf_op jit(solution)/shard_map/ppermute | solution.py:21
  436.6 2.1 collective-permute-start.1
  438.8 3.0 collective-permute-done.1
  441.8 0.1 pad_maximum_fusion
  441.9 0.1 pad_maximum_fusion.1
  442.1 0.6 concatenate.38
  442.8 0.9 fusion.47
  443.7 66.9 %all-gather.8.cloned.1.call-done = bf16[16,5,64,512]{3,0,2,1:T(8,128)(2,1)} async-done(((bf16[16,5,2,512]{3,0,2,1:T(8,128)(2,1)}), bf16[16,5,64,512]{3,0,2,1:T(8,128)(2,1)}) %all-gather.8.cloned.1.call-update) | async-done | bytes 5242896 | tf_op jit(solution)/shard_map/all_gather | solution.py:203
  510.6 5.5 fusion.26
  516.1 0.6 slice.103
  516.8 6.9 %fusion.32 = bf16[18,5,1,66,512]{4,0,3,1,2:T(8,128)(2,1)} fusion(bf16[16,5,64,512]{3,0,2,1:T(8,128)(2,1)S(1)} %fusion.26, bf16[1,5,64,512]{3,0,2,1:T(2,128)(2,1)S(1)} %slice.103), kind=kLoop, calls=%fused_computation.40 | loop fusion | flops 36495360 | bytes 11653120 | tf_op jit(solution)/shard_map/broadcast_in_dim | solution.py:209
  523.6 7.7 %pad.12 = bf16[18,5,1,72,512]{4,0,3,1,2:T(8,128)(2,1)} pad(bf16[18,5,1,66,512]{4,0,3,1,2:T(8,128)(2,1)} %fusion.32, bf16[]{:T(256)} %constant.54.clone.1), padding=0_0x0_0x0_0x0_6x0_0 | pad | bytes 12718082 | tf_op jit(solution)/shard_map/broadcast_in_dim | solution.py:209
  531.4 5.9 %copy.91 = bf16[18,5,1,8,9,512]{5,3,4,1,0,2:T(8,128)(2,1)S(1)} copy(bf16[18,5,1,8,9,512]{5,0,4,3,1,2:T(8,128)(2,1)} %bitcast.124) | data formatting | bytes 13271040 | tf_op jit(solution)/shard_map/conv_general_dilated | solution.py:208
  537.3 0.4 slice.104
  537.7 27.3 %fusion.43 = f32[16,3,8,9,16]{4,2,3,1,0:T(8,128)S(1)} fusion(bf16[16,3,3,3,512]{4,0,3,2,1:T(8,128)(2,1)S(1)} %copy-done.8, bf16[18,5,1,7,2,512]{5,3,4,1,0,2:T(8,128)(2,1)S(1)} %slice.104, bf16[18,5,1,8,9,512]{5,3,4,1,0,2:T(8,128)(2,1)S(1)} %copy.91, pred[8,9]{0,1:T(8,128)(4,1)S(1)} %copy-done.13), kind=kOutput, calls=%fused_computation.52 | convolution fusion | flops 1553209344 | bytes 8589384 | tf_op jit(solution)/shard_map/conv_general_dilated | solution.py:208
  564.9 0.3 copy.92
  565.3 1.6 slice-done
  566.8 0.3 fusion.49
  567.2 0.7 copy.93
  567.9 0.8 reshape.160
  (94 shorter events, 1.6 us)
Async XLA Ops:
  7.2 187.6 %copy-start = (bf16[128,3072]{1,0:T(8,128)(2,1)S(1)}, bf16[128,3072]{1,0:T(8,128)(2,1)}, u32[]{:S(2)}) copy-start(bf16[128,3072]{1,0:T(8,128)(2,1)} %param.26) | copy-start | bytes 2359300
  7.2 88.6 %all-gather.4.cloned.1.call-start = ((), (), s32[]{:S(2)}) async-start(), calls=%async_computation.5 | async-start | bytes 3244032 | tf_op jit(solution)/shard_map/all_gather | solution.py:63
  30.6 135.6 %all-gather.6.cloned.1.call-start = ((), (), s32[]{:S(2)}) async-start(), calls=%async_computation.6 | async-start | bytes 3244032 | tf_op jit(solution)/shard_map/all_gather | solution.py:64
  45.5 12.5 %all-to-all-start.1 = ((bf16[24,16,1,128]{3,0,2,1:T(8,128)(2,1)}), bf16[24,16,1,128]{3,0,2,1:T(8,128)(2,1)S(1)}, u32[]{:S(2)}, u32[]{:S(2)}) async-start(bf16[24,16,1,128]{3,0,2,1:T(8,128)(2,1)} %copy.76), calls=%async_computation.1 | async-start | bytes 196608 | tf_op jit(solution)/shard_map/all_to_all | solution.py:147
  49.0 360.6 %reduce-scatter.2.cloned.1.call-start = ((), (), s32[]{:S(2)}) async-start(), calls=%async_computation.7 | async-start | bytes 2506752 | tf_op jit(solution)/shard_map/reduce_scatter | solution.py:155
  194.6 2.4 copy-start.6
  194.6 2.6 copy-start.4
  194.6 215.0 %copy-start.2 = (bf16[2,1,1,24,3072]{4,3,2,1,0:T(8,128)(2,1)S(1)}, bf16[2,1,1,24,3072]{4,3,2,1,0:T(8,128)(2,1)}, u32[]{:S(2)}) copy-start(bf16[2,1,1,24,3072]{4,3,2,1,0:T(8,128)(2,1)} %param.18) | copy-start | bytes 884740
  194.6 215.0 %copy-start.3 = (bf16[1,1,24,3072]{3,2,1,0:T(8,128)(2,1)S(1)}, bf16[1,1,24,3072]{3,2,1,0:T(8,128)(2,1)}, u32[]{:S(2)}) copy-start(bf16[1,1,24,3072]{3,2,1,0:T(8,128)(2,1)} %param.17) | copy-start | bytes 442372
  194.7 215.0 %copy-start.5 = (f32[3072]{0:T(1024)S(1)}, f32[3072]{0:T(1024)}, u32[]{:S(2)}) copy-start(f32[3072]{0:T(1024)} %param.23) | copy-start | bytes 36868
  194.7 216.4 %copy-start.9 = (bf16[3072,64]{0,1:T(8,128)(2,1)S(1)}, bf16[3072,64]{0,1:T(8,128)(2,1)}, u32[]{:S(2)}) copy-start(bf16[3072,64]{0,1:T(8,128)(2,1)} %param.27) | copy-start | bytes 1179652
  194.7 216.4 %copy-start.10 = (f32[3072]{0:T(1024)S(1)}, f32[3072]{0:T(1024)}, u32[]{:S(2)}) copy-start(f32[3072]{0:T(1024)} %param.24) | copy-start | bytes 36868
  194.7 216.4 %copy-start.12 = (f32[64]{0:T(128)S(1)}, f32[64]{0:T(128)}, u32[]{:S(2)}) copy-start(f32[64]{0:T(128)} %param.28) | copy-start | bytes 772
  197.0 245.8 %copy-start.7 = (bf16[3,3,3,16,512]{4,3,2,1,0:T(8,128)(2,1)S(1)}, bf16[3,3,3,16,512]{4,3,2,1,0:T(8,128)(2,1)}, u32[]{:S(2)}) copy-start(bf16[3,3,3,16,512]{4,3,2,1,0:T(8,128)(2,1)} %param.29) | copy-start | bytes 1327108
  197.0 245.8 %copy-start.11 = (f32[512]{0:T(512)S(1)}, f32[512]{0:T(512)}, u32[]{:S(2)}) copy-start(f32[512]{0:T(512)} %param.30) | copy-start | bytes 6148
  410.8 105.3 %copy-start.1 = (bf16[24,3072]{1,0:T(8,128)(2,1)}, bf16[24,3072]{1,0:T(8,128)(2,1)S(1)}, u32[]{:S(2)}) copy-start(bf16[24,3072]{1,0:T(8,128)(2,1)S(1)} %get-tuple-element.112) | copy-start | bytes 442372
  412.8 13.8 %all-to-all-start.3 = ((bf16[1,16,7,32]{3,2,0,1:T(8,128)(2,1)}), bf16[1,16,7,32]{3,2,0,1:T(8,128)(2,1)S(1)}, u32[]{:S(2)}, u32[]{:S(2)}) async-start(bf16[1,16,7,32]{3,2,0,1:T(8,128)(2,1)} %bitcast.21), calls=%async_computation.4 | async-start | bytes 65536 | tf_op jit(solution)/shard_map/all_to_all | solution.py:191
  417.8 92.8 %all-gather.8.cloned.1.call-start = ((), (), s32[]{:S(2)}) async-start(), calls=%async_computation.8 | async-start | bytes 5406720 | tf_op jit(solution)/shard_map/all_gather | solution.py:203
  426.9 11.9 %collective-permute-start = (bf16[16,7,1,16]{3,0,2,1:T(8,128)(2,1)S(1)}, bf16[16,7,1,16]{3,0,2,1:T(8,128)(2,1)S(1)}, u32[]{:S(2)}, u32[]{:S(2)}) collective-permute-start(bf16[16,7,1,16]{3,0,2,1:T(8,128)(2,1)S(1)} %copy.103), channel_id=1, source_target_pairs={{0,1},{1,2},{2,3},{3,4},{4,5},{5,6},{6,7},{7,8},{8,9},{9,10},{10,1... | collective-permute-start | bytes 10760 | tf_op jit(solution)/shard_map/ppermute | solution.py:21
  436.6 5.2 collective-permute-start.1
  531.4 6.3 %copy-start.8 = (bf16[16,3,3,3,512]{4,0,3,2,1:T(8,128)(2,1)S(1)}, bf16[16,3,3,3,512]{4,0,3,2,1:T(8,128)(2,1)}, u32[]{:S(2)}) copy-start(bf16[16,3,3,3,512]{4,0,3,2,1:T(8,128)(2,1)} %param.31) | copy-start | bytes 1327108
  531.4 6.3 %copy-start.13 = (pred[8,9]{0,1:T(8,128)(4,1)S(1)}, pred[8,9]{0,1:T(8,128)(4,1)}, u32[]{:S(2)}) copy-start(pred[8,9]{0,1:T(8,128)(4,1)} %constant.74) | copy-start | bytes 220
  564.9 1.9 slice-start
Sparse Core Ops, SparseCore 0:
  30.7 65.0 all-gather.3
  97.9 68.2 all-gather.5
  197.2 212.4 reduce-scatter.1
  443.8 66.7 all-gather.7
where the time goes:
time: 576 us; the launch traced here: 575 us
  waiting for transfers between devices  408 us (71%)
  matrix products  55.1 us (10%)
  blocking collectives  34.6 us (6%)
  local copies, waits for them, and re-layouts  24.3 us (4%)
  starting transfers between devices  20.4 us (4%)
  other arithmetic  18.2 us (3%)
  between operations  14.3 us (2%)
    reduce_scatter x1, waiting for transfers between devices, per_device(): lax.psum_scatter(jnp.dot(flat_attended, out_weight, preferred_element_typ...  212 us
    all_gather x1, waiting for transfers between devices, attend(): value_piece = lax.all_gather(value_all, 'sp', axis=0, tiled=True)  70.4 us
    all_gather x1, waiting for transfers between devices, per_device(): first_full = lax.all_gather(first_part, 'sp', axis=2, tiled=True)  66.9 us
    all_gather x1, waiting for transfers between devices, attend(): key_piece = lax.all_gather(key_all, 'sp', axis=0, tiled=True)  37.9 us
    conv_general_dilated x1, matrix products, per_device(): lax.conv_general_dilated(act_pad[None], second_weight, (1, 1, 1), 'VALID'...  27.3 us
    all_to_all x1, blocking collectives, per_device(): lax.all_to_all(split_heads(attn_keys), 'grp', split_axis=1, concat_axis=0...  22.3 us
    dot_general x8, matrix products, online_update(): jnp.einsum('api,iak->apk', weights_now.astype(jnp.bfloat16), value_rows,...  12.5 us
    all_to_all x1, blocking collectives, per_device(): lax.all_to_all(split_heads(values), 'grp', split_axis=1, concat_axis=0, t...  12.3 us
  transfers between devices with their start and end apart: 8, of which 7 were waited for; matrix products, arithmetic and copies ran while one was open for 0% of the time, Pallas kernels for 0%

commit v1 on v0

v1 whole, which is shorter than its diff:
```python
import math

import jax
import jax.numpy as jnp
from jax import lax
from jax.experimental import pallas as pl
from jax.experimental.pallas import tpu as pltpu
from jax.sharding import Mesh, PartitionSpec as P

HD = 128
HEADS = 16
F32 = jnp.float32
BF16 = jnp.bfloat16
MIB = 1 << 20

TOK = 24
FRAMES = 16
PIX = 1024
SUB = 128

VMEM = pl.BlockSpec(memory_space=pltpu.VMEM)
SMEM = pl.BlockSpec(memory_space=pltpu.SMEM)

GRP = ("h", "z")
COL = ("ya", "yb", "l", "c")


def dot(a, b, contract):
    return lax.dot_general(a, b, ((contract[0], contract[1]), ((), ())), preferred_element_type=F32)


def pack_kernel(q_ref, k_ref, v_ref, out_ref):
    for g in range(HEADS):
        cols = slice(g * HD, (g + 1) * HD)
        out_ref[g, :, 0:HD] = q_ref[:, cols]
        out_ref[g, :, HD : 2 * HD] = k_ref[:, cols]
        out_ref[g, :, 2 * HD : 3 * HD] = v_ref[:, cols]


def pack(q, k, v):
    return pl.pallas_call(
        pack_kernel,
        out_shape=jax.ShapeDtypeStruct((HEADS, TOK, 3 * HD), BF16),
        in_specs=[VMEM] * 3,
        out_specs=VMEM,
    )(q, k, v)


def attend_kernel(q_ref, kv_ref, out_ref):
    scale = math.log2(math.e) / math.sqrt(HD)
    rows = q_ref.shape[1]
    keys = kv_ref[:, 0:HD]
    vals = kv_ref[:, HD : 2 * HD]
    outs, logs = [], []
    for i in range(rows // SUB):
        q = q_ref[0, i * SUB : (i + 1) * SUB, :]
        s = dot(q, keys, ((1,), (1,)))
        top = jnp.max(s, axis=1, keepdims=True)
        p = jnp.exp2(s * scale - top * scale)
        total = jnp.sum(p, axis=1, keepdims=True)
        o = dot(p.astype(BF16), vals, ((1,), (0,)))
        outs.append(o / total)
        logs.append(top * scale + jnp.log2(total))
    o = jnp.concatenate(outs, axis=0).reshape(2, 8, TOK, HD)
    log = jnp.concatenate(logs, axis=0)
    hi = log.astype(BF16).astype(F32)
    mid = (log - hi).astype(BF16).astype(F32)
    lo = log - hi - mid
    hi, mid, lo = (x.reshape(2, 8, TOK, 1) for x in (hi, mid, lo))
    token = lax.broadcasted_iota(jnp.int32, (2 * TOK, HD), 0)
    lane = lax.broadcasted_iota(jnp.int32, (2 * TOK, HD), 1)
    base = lane - lax.rem(token, 3) * 3
    row = lax.broadcasted_iota(jnp.int32, (16, 2 * TOK), 0)
    spot = lax.broadcasted_iota(jnp.int32, (16, 2 * TOK), 1)
    pick = jnp.where(lax.div(spot, 3) == row, 1.0, 0.0).astype(BF16)
    for z in range(8):
        piece = [jnp.concatenate([x[0, z], x[1, z]], axis=0) for x in (hi, mid, lo)]
        spread = jnp.where(
            base == 0,
            piece[0],
            jnp.where(base == 1, piece[1], jnp.where(base == 2, piece[2], 0.0)),
        )
        stats = dot(pick, spread.astype(BF16), ((1,), (0,)))
        out_ref[z, 0] = jnp.concatenate([o[0, z], o[1, z], stats], axis=0).astype(BF16)


def attend(q, kv):
    return pl.pallas_call(
        attend_kernel,
        grid=(4,),
        out_shape=jax.ShapeDtypeStruct((8, 4, 64, HD), BF16),
        in_specs=[
            pl.BlockSpec((1, FRAMES * TOK, HD), lambda i: (i, 0, 0)),
            pl.BlockSpec(kv.shape, lambda i: (0, 0)),
        ],
        out_specs=pl.BlockSpec((8, 1, 64, HD), lambda i: (0, i, 0, 0)),
        compiler_params=pltpu.CompilerParams(vmem_limit_bytes=48 * MIB),
    )(q, kv)


def project_kernel(h_ref, parts_ref, weight_ref, keep_ref, send_ref, att_ref, sum_ref):
    @pl.when(pl.program_id(0) == 0)
    def join():
        token = lax.broadcasted_iota(jnp.int32, (2 * TOK, HD), 0)
        lane = lax.broadcasted_iota(jnp.int32, (2 * TOK, HD), 1)
        base = lane - lax.rem(token, 3) * 3
        mine = (base >= 0) & (base < 3)
        spot = lax.broadcasted_iota(jnp.int32, (2 * TOK, 16), 0)
        row = lax.broadcasted_iota(jnp.int32, (2 * TOK, 16), 1)
        pick = jnp.where(lax.div(spot, 3) == row, 1.0, 0.0).astype(BF16)
        for z in range(8):
            logs = []
            for j in range(4):
                spread = dot(pick, parts_ref[z, j, 48:64, :], ((1,), (0,)))
                logs.append(jnp.sum(jnp.where(mine, spread, 0.0), axis=1, keepdims=True))
            top = jnp.maximum(jnp.maximum(logs[0], logs[1]), jnp.maximum(logs[2], logs[3]))
            shares = [jnp.exp2(x - top) for x in logs]
            total = (shares[0] + shares[1]) + (shares[2] + shares[3])
            att = jnp.zeros((2 * TOK, HD), F32)
            for j in range(4):
                att = att + parts_ref[z, j, 0:48, :].astype(F32) * (shares[j] / total)
            att_ref[:, z * HD : (z + 1) * HD] = att.astype(BF16)

    sum_ref[...] = dot(att_ref[...], weight_ref[...], ((1,), (0,)))
    h = h_ref[0]
    keep_ref[...] = sum_ref[pl.ds(pl.multiple_of(h * TOK, 8), TOK), :]
    send_ref[...] = sum_ref[pl.ds(pl.multiple_of((1 - h) * TOK, 8), TOK), :].astype(BF16)


def project(h, parts, weight):
    depth, width = weight.shape
    block = 768
    return pl.pallas_call(
        project_kernel,
        grid=(width // block,),
        out_shape=(
            jax.ShapeDtypeStruct((TOK, width), F32),
            jax.ShapeDtypeStruct((TOK, width), BF16),
        ),
        in_specs=[
            SMEM,
            pl.BlockSpec(parts.shape, lambda i: (0, 0, 0, 0)),
            pl.BlockSpec((depth, block), lambda i: (0, i)),
        ],
        out_specs=(
            pl.BlockSpec((TOK, block), lambda i: (0, i)),
            pl.BlockSpec((TOK, block), lambda i: (0, i)),
        ),
        scratch_shapes=[pltpu.VMEM((2 * TOK, depth), BF16), pltpu.VMEM((2 * TOK, block), F32)],
        compiler_params=pltpu.CompilerParams(vmem_limit_bytes=32 * MIB),
    )(h, parts, weight)


def norm_kernel(
    keep_ref, recv_ref, res_ref, cached_ref, use_ref, gate_ref, shift_ref, scale_ref, fw_ref, fb_ref,
    stream_ref, out_ref,
):
    eye = lax.broadcasted_iota(jnp.int32, (TOK, TOK), 0) == lax.broadcasted_iota(
        jnp.int32, (TOK, TOK), 1
    )
    mixed = res_ref[...].astype(F32)
    for b in range(2):
        used = use_ref[b : b + 1, :].astype(F32)
        column = jnp.sum(jnp.where(eye, used, 0.0), axis=1, keepdims=True)
        mixed = mixed + column * cached_ref[b].astype(F32)
    projected = keep_ref[...] + recv_ref[...].astype(F32)
    stream = (mixed + gate_ref[...] * projected).astype(BF16)
    stream_ref[...] = stream
    x = stream.astype(F32)
    center = jnp.mean(x, axis=1, keepdims=True)
    off = x - center
    spread = jnp.mean(off * off, axis=1, keepdims=True)
    modulated = off * lax.rsqrt(spread + 1e-6) * (1.0 + scale_ref[...]) + shift_ref[...]
    latent = dot(modulated.astype(BF16), fw_ref[...], ((1,), (0,))) + fb_ref[...]
    latent = latent.astype(BF16)
    band = lax.broadcasted_iota(jnp.int32, (FRAMES, TOK), 0)
    source = lax.broadcasted_iota(jnp.int32, (FRAMES, TOK), 1)
    first = lax.div(3 * band, 2) - 1
    pieces = [
        dot(jnp.where(source == first + k, 1.0, 0.0).astype(BF16), latent, ((1,), (0,)))
        for k in range(4)
    ]
    window = jnp.concatenate(pieces, axis=1)
    out_ref[...] = jnp.broadcast_to(window[:, None, :], (FRAMES, 32, 256)).astype(BF16)


def norm(keep, recv, res, cached, use, gate, shift, scale, fw, fb):
    return pl.pallas_call(
        norm_kernel,
        out_shape=(
            jax.ShapeDtypeStruct(res.shape, BF16),
            jax.ShapeDtypeStruct((FRAMES, 32, 256), BF16),
        ),
        in_specs=[VMEM] * 10,
        out_specs=(VMEM, VMEM),
        compiler_params=pltpu.CompilerParams(vmem_limit_bytes=32 * MIB),
    )(keep, recv, res, cached, use, gate, shift, scale, fw, fb)


def frames_back(x, count, lane):
    if count == 0:
        return x
    moved = pltpu.roll(x, 64 * count, 1)
    start = x[:, 0:128]
    start = jnp.where(lane[:, 0:128] < 64, start, pltpu.roll(start, 64, 1))
    width = 128
    head = jnp.where(lane[:, 0:width] < 64 * count, start, moved[:, 0:width])
    return jnp.concatenate([head, moved[:, width:]], axis=1)


def column_shift(x, by, place):
    if by == 0:
        return x
    moved = pltpu.roll(x, (-by) % PIX, 1)
    edge = 63 if by == 1 else 0
    return jnp.where(place == edge, 0.0, moved)


def conv_kernel(place_ref, lat_ref, w1_ref, b1_ref, w2_ref, out_ref, taps_ref, w1t_ref, first_ref, acc_ref):
    band = place_ref[0]
    lanes = place_ref[1]
    w1t_ref[...] = jnp.transpose(w1_ref[...].astype(F32)).astype(BF16)
    flat = jnp.transpose(lat_ref[...].astype(F32))
    lane16 = lax.broadcasted_iota(jnp.int32, (16, PIX), 1)
    place16 = lax.rem(lane16, 64)
    source = lax.broadcasted_iota(jnp.int32, (128, 128), 0)
    target = lax.broadcasted_iota(jnp.int32, (128, 128), 1)
    wanted = (
        lax.rem(target, 2) * 64 + lax.div(target, 64) * 32 + lax.div(lax.rem(target, 64), 2)
    )
    weave = jnp.where(source == wanted, 1.0, 0.0).astype(BF16)
    rows_b = [
        jnp.concatenate([flat[r * 32 + b * 16 : r * 32 + b * 16 + 16] for r in range(8)], axis=0)
        for b in range(2)
    ]
    blocks = []
    for n in range(8):
        both = jnp.concatenate([x[:, n * 64 : (n + 1) * 64] for x in rows_b], axis=1)
        blocks.append(dot(both.astype(BF16), weave, ((1,), (0,))))
    latent = jnp.concatenate(blocks, axis=1)
    for r in range(8):
        row = latent[r * 16 : r * 16 + 16]
        for b in range(3):
            moved = column_shift(row, b - 1, place16)
            for t in range(3):
                at = r * 48 + b * 16
                taps_ref[t, at : at + 16, :] = frames_back(moved, 2 - t, lane16).astype(BF16)
    acc_ref[...] = jnp.zeros_like(acc_ref)
    odd = lax.rem(band, 2)
    bias = b1_ref[...]
    for r in range(5):
        at = pl.multiple_of((odd + r) * 48, 16)
        patches = jnp.concatenate([taps_ref[t, pl.ds(at, 144), :] for t in range(3)], axis=0)
        first = dot(w1t_ref[...], patches, ((1,), (0,))) + bias
        height = 3 * band - 1 + r
        inside = jnp.where((height >= 0) & (height < 48), 1.0, 0.0)
        v = (first * inside).astype(BF16).astype(F32)
        if 1 <= r <= 3:
            first_ref[...] = v
            own = first_ref[pl.ds(pl.multiple_of(lanes * 16, 16), 16), :]
            acc_ref[r - 1, 2, 16:32, :] += own
        half = 0.5 * v
        act = (half * jnp.tanh(half) + half).astype(BF16)
        z = dot(w2_ref[...], act, ((1,), (0,)))
        for a in range(3):
            o = r - a
            if 0 <= o < 3:
                for t in range(3):
                    acc_ref[o, t] += z[(t * 3 + a) * 48 : (t * 3 + a + 1) * 48]
    for o in range(3):
        total = None
        for t in range(3):
            u = acc_ref[o, t, 16:32, :]
            u = u + column_shift(acc_ref[o, t, 0:16, :], -1, place16)
            u = u + column_shift(acc_ref[o, t, 32:48, :], 1, place16)
            u = frames_back(u, 2 - t, lane16)
            total = u if total is None else total + u
        out_ref[o] = total.astype(BF16)


def conv(place, lat, w1, b1, w2):
    return pl.pallas_call(
        conv_kernel,
        out_shape=jax.ShapeDtypeStruct((3, 16, PIX), BF16),
        in_specs=[SMEM] + [VMEM] * 4,
        out_specs=VMEM,
        scratch_shapes=[
            pltpu.VMEM((3, 8 * 48, PIX), BF16),
            pltpu.VMEM((512, 432), BF16),
            pltpu.VMEM((512, PIX), F32),
            pltpu.VMEM((3, 3, 48, PIX), F32),
        ],
        compiler_params=pltpu.CompilerParams(vmem_limit_bytes=56 * MIB),
    )(place, lat, w1, b1, w2)


def per_device(
    residual_in,
    cached,
    use_cached,
    queries,
    attn_keys,
    values,
    gate_mod,
    shift_mod,
    scale_mod,
    out_weight,
    final_weight,
    final_bias,
    first_weight,
    first_bias,
    second_weight,
):
    model_width = residual_in.shape[-1]
    channels = first_weight.shape[-1]
    weight = lax.all_gather(out_weight, "z", axis=0, tiled=True)

    packed = pack(*(x.reshape(TOK, HEADS * HD) for x in (queries, attn_keys, values)))
    moved = lax.all_to_all(packed, GRP, split_axis=0, concat_axis=0, tiled=True)
    moved = moved.reshape(FRAMES * TOK, 3 * HD)
    kv = jnp.broadcast_to(moved[None, :, HD:], (8, FRAMES * TOK, 2 * HD))
    kv = lax.all_to_all(kv, ("yb", "l", "c"), split_axis=0, concat_axis=0, tiled=True)
    q = jnp.broadcast_to(moved[None, :, :HD], (4, FRAMES * TOK, HD))
    q = lax.all_to_all(q, "ya", split_axis=0, concat_axis=0, tiled=True)
    parts = attend(q, kv.reshape(8 * FRAMES * TOK, 2 * HD))
    parts = lax.all_to_all(
        parts.reshape(32, 64, HD), ("z", "ya"), split_axis=0, concat_axis=0, tiled=True
    )
    h = lax.axis_index("h").astype(jnp.int32)
    keep, send = project(h.reshape(1), parts.reshape(8, 4, 64, HD), weight)
    recv = lax.ppermute(send, "h", [(0, 1), (1, 0)])
    stream, windows = norm(
        keep,
        recv,
        residual_in.reshape(TOK, model_width),
        cached.reshape(2, TOK, model_width),
        use_cached.reshape(2, TOK),
        gate_mod[None, :],
        shift_mod[None, :],
        scale_mod[None, :],
        final_weight,
        final_bias[None, :],
    )
    lat = lax.all_to_all(
        windows.reshape(512, 256), GRP + COL, split_axis=0, concat_axis=0, tiled=True
    )
    place = jnp.stack([lax.axis_index(GRP), lax.axis_index(COL)]).astype(jnp.int32)
    w2 = jnp.transpose(second_weight, (1, 2, 3, 0, 4)).reshape(27 * 16, channels)
    out = conv(place, lat, first_weight.reshape(27 * 16, channels), first_bias[:, None], w2)
    return stream.reshape(residual_in.shape), jnp.transpose(out, (1, 0, 2))


def solution(mesh):
    fine = Mesh(mesh.devices.reshape(2, 8, 4, 2, 2, 2), GRP + COL)
    return jax.shard_map(
        per_device,
        mesh=fine,
        in_specs=(
            P(GRP, COL, None, None),
            P(None, GRP, COL, None, None),
            P(None, GRP, COL, None),
            P(GRP, COL, None, None),
            P(GRP, COL, None, None),
            P(GRP, COL, None, None),
            P(),
            P(),
            P(),
            P(GRP, None),
            P(),
            P(),
            P(),
            P(),
            P(COL, None, None, None, None),
        ),
        out_specs=(P(GRP, COL, None, None), P(COL, GRP, None)),
        check_vma=False,
    )
```

time: 576 us -> 176 us (0.31)
  waiting for transfers between devices: 408 us -> 43.2 us
  matrix products: 55.1 us -> 0 us
  Pallas kernels: 0 us -> 24.5 us
  local copies, waits for them, and re-layouts: 24.3 us -> 7.19 us
  other arithmetic: 18.2 us -> 1.46 us
  blocking collectives: 34.6 us -> 51.2 us
  starting transfers between devices: 20.4 us -> 33.3 us
    reduce_scatter x1 -> x0, waiting for transfers between devices: 212 us -> none  [per_device(): lax.psum_scatter(jnp.dot(flat_attended, out_weight, preferred_element_typ...]
    all_gather x3 -> x1, waiting for transfers between devices: 175 us -> 0.01 us  [per_device(): weight = lax.all_gather(out_weight, 'z', axis=0, tiled=True)]
    dot_general x19 -> x0, matrix products: 27.8 us -> none  [the longest x8 12.5 us: online_update(): jnp.einsum('api,iak->apk', weights_now.astype(jnp.bfloat16), value_rows,...]
    conv_general_dilated x1 -> x0, matrix products: 27.3 us -> none  [per_device(): lax.conv_general_dilated(act_pad[None], second_weight, (1, 1, 1), 'VALID'...]
    pallas_call x0 -> x5, Pallas kernels: none -> 24.5 us  [the longest x1 10.7 us: attend(): pl.pallas_call(attend_kernel, grid=(4,), out_shape=jax.ShapeDtypeStruct((...]
    all_to_all x2 -> x3, starting transfers between devices: 8.48 us -> 30 us  [the longest x1 16.3 us: per_device(): lax.all_to_all(windows.reshape(512, 256), GRP + COL, split_axis=0, concat...]
    all_to_all x2 -> x3, waiting for transfers between devices: 17.7 us -> 38.8 us  [the longest x1 15.1 us: per_device(): lax.all_to_all(windows.reshape(512, 256), GRP + COL, split_axis=0, concat...]
    all_to_all x2, blocking collectives: 34.6 us -> 51.2 us  [the longest x1 27.1 us: per_device(): lax.all_to_all(kv, ('yb', 'l', 'c'), split_axis=0, concat_axis=0, tiled=T...]
  transfers between devices with their start and end apart: 8 -> 5, of which waited for: 7 -> 4; matrix products, arithmetic and copies ran while one was open for 0% -> 2% of each run, Pallas kernels for 0% -> 7%
where the time goes in v1:
time: 176 us; the launch traced here: 175 us
  blocking collectives  51.2 us (29%)
  waiting for transfers between devices  43.2 us (25%)
  starting transfers between devices  33.3 us (19%)
  Pallas kernels  24.5 us (14%)
  between operations  14.2 us (8%)
  local copies, waits for them, and re-layouts  7.19 us (4%)
    all_to_all x1, blocking collectives, per_device(): lax.all_to_all(kv, ('yb', 'l', 'c'), split_axis=0, concat_axis=0, tiled=T...  27.1 us
    all_to_all x1, blocking collectives, per_device(): moved = lax.all_to_all(packed, GRP, split_axis=0, concat_axis=0, tiled=True)  24.1 us
    all_to_all x1, starting transfers between devices, per_device(): lax.all_to_all(windows.reshape(512, 256), GRP + COL, split_axis=0, concat...  16.3 us
    all_to_all x1, waiting for transfers between devices, per_device(): lax.all_to_all(windows.reshape(512, 256), GRP + COL, split_axis=0, concat...  15.1 us
    all_to_all x1, waiting for transfers between devices, per_device(): lax.all_to_all(parts.reshape(32, 64, HD), ('z', 'ya'), split_axis=0, conc...  14.9 us
    pallas_call x1, Pallas kernels, attend(): pl.pallas_call(attend_kernel, grid=(4,), out_shape=jax.ShapeDtypeStruct((...  10.7 us
    all_to_all x1, waiting for transfers between devices, per_device(): q = lax.all_to_all(q, 'ya', split_axis=0, concat_axis=0, tiled=True)  8.82 us
    pallas_call x1, Pallas kernels, conv(): pl.pallas_call(conv_kernel, out_shape=jax.ShapeDtypeStruct((3, 16, PIX),...  8.62 us
  transfers between devices with their start and end apart: 5, of which 4 were waited for; matrix products, arithmetic and copies ran while one was open for 2% of the time, Pallas kernels for 7%

profile of v1, /device:TPU:1, one launch (start us, length us, event | category | flops | bytes accessed | tf_op | source)
XLA Modules:
  0.0 175.0 jit_solution(8534164910259398766)
XLA Ops:
  7.2 0.0 all-gather.2.cloned.1.call-start
  7.2 0.7 all-gather.2.cloned.1.call-update
  7.9 1.8 %shard_map.158 = bf16[16,24,384]{2,1,0:T(8,128)(2,1)} custom-call(bf16[24,2048]{1,0:T(8,128)(2,1)} %bitcast.43, bf16[24,2048]{1,0:T(8,128)(2,1)} %bitcast.44, bf16[24,2048]{1,0:T(8,128)(2,1)} %bitcast.45), custom_call_target="tpu_custom_call" | custom-call | tf_op jit(solution)/shard_map/pallas_call | solution.py:41
  9.7 24.1 %all_to_all.31 = bf16[16,24,384]{2,1,0:T(8,128)(2,1)S(1)} all-to-all(bf16[16,24,384]{2,1,0:T(8,128)(2,1)} %shard_map.158), channel_id=1, replica_groups=mesh['h'=2,'z'=8,'ya'=4,'yb'=2,'l'=2,'c'=2] {'h','z'}, dimensions={0} | all-to-all | bytes 589824 | tf_op jit(solution)/shard_map/all_to_all | solution.py:319
  33.8 0.8 broadcast_in_dim.27
  34.6 6.8 %all-to-all-start.1 = ((bf16[4,384,128]{2,1,0:T(8,128)(2,1)}), bf16[4,384,128]{2,1,0:T(8,128)(2,1)S(1)}, u32[]{:S(2)}, u32[]{:S(2)}) async-start(bf16[4,384,128]{2,1,0:T(8,128)(2,1)} %broadcast_in_dim.27), calls=%async_computation.1 | async-start | bytes 786432 | tf_op jit(solution)/shard_map/all_to_all | solution.py:324
  41.4 8.8 %all-to-all-done.1.q_ref = bf16[4,384,128]{2,1,0:T(8,128)(2,1)S(1)} async-done(((bf16[4,384,128]{2,1,0:T(8,128)(2,1)}), bf16[4,384,128]{2,1,0:T(8,128)(2,1)S(1)}, u32[]{:S(2)}, u32[]{:S(2)}) %all-to-all-start.1) | async-done | bytes 393248 | tf_op jit(solution)/shard_map/all_to_all | solution.py:324
  50.2 0.1 broadcast_in_dim.28
  50.3 27.1 %all_to_all.32 = bf16[8,384,256]{2,1,0:T(8,128)(2,1)S(1)} all-to-all(bf16[8,384,256]{2,1,0:T(8,128)(2,1)S(1)} %broadcast_in_dim.28), channel_id=1, replica_groups=mesh['h'=2,'z'=8,'ya'=4,'yb'=2,'l'=2,'c'=2] {'yb','l','c'}, dimensions={0} | all-to-all | bytes 3145728 | tf_op jit(solution)/shard_map/all_to_all | solution.py:322
  77.4 10.7 %shard_map.159 = bf16[8,4,64,128]{3,2,1,0:T(8,128)(2,1)} custom-call(bf16[4,384,128]{2,1,0:T(8,128)(2,1)S(1)} %all-to-all-done.1.q_ref, bf16[3072,256]{1,0:T(8,128)(2,1)S(1)} %bitcast.28), custom_call_target="tpu_custom_call" | custom-call | tf_op jit(solution)/shard_map/pallas_call | solution.py:88
  88.1 6.9 %all-to-all-start.3 = ((bf16[32,64,128]{2,1,0:T(8,128)(2,1)}), bf16[32,64,128]{2,1,0:T(8,128)(2,1)S(1)}, u32[]{:S(2)}, u32[]{:S(2)}) async-start(bf16[32,64,128]{2,1,0:T(8,128)(2,1)} %bitcast.6), calls=%async_computation.3 | async-start | bytes 1048576 | tf_op jit(solution)/shard_map/all_to_all | solution.py:326
  95.0 14.9 %all-to-all-done.3 = bf16[32,64,128]{2,1,0:T(8,128)(2,1)S(1)} async-done(((bf16[32,64,128]{2,1,0:T(8,128)(2,1)}), bf16[32,64,128]{2,1,0:T(8,128)(2,1)S(1)}, u32[]{:S(2)}, u32[]{:S(2)}) %all-to-all-start.3) | async-done | bytes 524320 | tf_op jit(solution)/shard_map/all_to_all | solution.py:326
  109.9 0.0 all-gather.2.cloned.1.call-done.weight_ref
  109.9 0.0 copy-start
  109.9 2.8 %copy-done = bf16[1024,3072]{1,0:T(8,128)(2,1)S(1)} copy-done((bf16[1024,3072]{1,0:T(8,128)(2,1)S(1)}, bf16[1024,3072]{1,0:T(8,128)(2,1)}, u32[]{:S(2)}) %copy-start) | copy-done | bytes 6291480
  112.7 0.0 copy-start.8
  112.7 0.0 copy-start.1
  112.7 0.0 copy-start.2
  112.7 0.0 copy-start.3
  112.7 0.0 copy-start.4
  112.7 0.0 copy-start.5
  112.7 0.0 copy-start.6
  112.8 0.0 copy-start.7
  112.8 2.6 %shard_map.160 = (f32[24,3072]{1,0:T(8,128)S(1)}, bf16[24,3072]{1,0:T(8,128)(2,1)S(1)}) custom-call(s32[1]{0:T(128)} %bitcast.h_ref, bf16[8,4,64,128]{3,2,1,0:T(8,128)(2,1)S(1)} %bitcast.29, bf16[1024,3072]{1,0:T(8,128)(2,1)S(1)} %copy-done), custom_call_target="tpu_custom_call" | custom-call | tf_op jit(solution)/shard_map/pallas_call | solution.py:133
  115.4 3.2 %collective-permute-start = (bf16[24,3072]{1,0:T(8,128)(2,1)S(1)}, bf16[24,3072]{1,0:T(8,128)(2,1)S(1)}, u32[]{:S(2)}, u32[]{:S(2)}) collective-permute-start(bf16[24,3072]{1,0:T(8,128)(2,1)S(1)} %get-tuple-element.7), channel_id=1, source_target_pairs={{0,256},{256,0},{1,257},{257,1},{2,258},{258,2},{3,259},{259,3},{4... | collective-permute-start | bytes 442376 | tf_op jit(solution)/shard_map/ppermute | solution.py:331
  118.6 0.0 copy-done.8
  118.6 0.4 copy.23.fw_ref
  119.0 3.8 %collective-permute-done.recv_ref = bf16[24,3072]{1,0:T(8,128)(2,1)S(1)} collective-permute-done((bf16[24,3072]{1,0:T(8,128)(2,1)S(1)}, bf16[24,3072]{1,0:T(8,128)(2,1)S(1)}, u32[]{:S(2)}, u32[]{:S(2)}) %collective-permute-start) | collective-permute-done | bytes 147488 | tf_op jit(solution)/shard_map/ppermute | solution.py:331
  122.8 0.0 copy-done.1
  122.8 0.0 copy-done.2
  122.8 0.0 copy-done.3
  122.8 0.0 copy-done.4
  122.8 0.0 copy-done.5
  122.8 0.0 copy-done.6
  122.8 0.0 copy-done.7
  122.8 0.0 copy-start.9
  122.8 0.9 shard_map.161
  123.7 0.6 broadcast.2
  124.3 0.9 reduce
  125.1 0.8 reshape.66
  125.9 16.3 %all-to-all-start.4 = ((bf16[512,2,128]{2,1,0:T(2,128)(2,1)}), bf16[512,2,128]{2,1,0:T(2,128)(2,1)S(1)}, u32[]{:S(2)}, u32[]{:S(2)}) async-start(bf16[512,2,128]{2,1,0:T(2,128)(2,1)} %reshape.66), calls=%async_computation.4 | async-start | bytes 524288 | tf_op jit(solution)/shard_map/all_to_all | solution.py:344
  142.2 0.0 copy-done.9
  142.2 0.8 copy.25.b1_ref
  143.0 0.6 pad_add_fusion.place_ref
  143.6 15.1 %all-to-all-done.4 = bf16[512,2,128]{2,1,0:T(2,128)(2,1)S(1)} async-done(((bf16[512,2,128]{2,1,0:T(2,128)(2,1)}), bf16[512,2,128]{2,1,0:T(2,128)(2,1)S(1)}, u32[]{:S(2)}, u32[]{:S(2)}) %all-to-all-start.4) | async-done | bytes 262176 | tf_op jit(solution)/shard_map/all_to_all | solution.py:344
  158.7 0.1 reshape.67
  158.8 0.7 copy.28
  159.6 8.6 %shard_map.162 = bf16[3,16,1024]{2,1,0:T(8,128)(2,1)} custom-call(s32[2]{0:T(128)} %pad_add_fusion.place_ref, bf16[512,256]{1,0:T(8,128)(2,1)} %bitcast.40, bf16[432,512]{1,0:T(8,128)(2,1)} %bitcast.41, f32[512,1]{1,0:T(8,128)} %copy.25.b1_ref, bf16[432,512]{1,0:T(8,128)(2,1)} %bitcast.42), custom_call_target="tpu_custom_call" | custom-call | tf_op jit(solution)/shard_map/pallas_call | solution.py:282
  (2 shorter events, 0.0 us)
Async XLA Ops:
  7.2 102.8 %all-gather.2.cloned.1.call-start = ((), (), s32[]{:S(2)}) async-start(), calls=%async_computation.5 | async-start | bytes 7077888 | tf_op jit(solution)/shard_map/all_gather | solution.py:316
  34.6 15.7 %all-to-all-start.1 = ((bf16[4,384,128]{2,1,0:T(8,128)(2,1)}), bf16[4,384,128]{2,1,0:T(8,128)(2,1)S(1)}, u32[]{:S(2)}, u32[]{:S(2)}) async-start(bf16[4,384,128]{2,1,0:T(8,128)(2,1)} %broadcast_in_dim.27), calls=%async_computation.1 | async-start | bytes 786432 | tf_op jit(solution)/shard_map/all_to_all | solution.py:324
  88.1 21.8 %all-to-all-start.3 = ((bf16[32,64,128]{2,1,0:T(8,128)(2,1)}), bf16[32,64,128]{2,1,0:T(8,128)(2,1)S(1)}, u32[]{:S(2)}, u32[]{:S(2)}) async-start(bf16[32,64,128]{2,1,0:T(8,128)(2,1)} %bitcast.6), calls=%async_computation.3 | async-start | bytes 1048576 | tf_op jit(solution)/shard_map/all_to_all | solution.py:326
  109.9 2.8 %copy-start = (bf16[1024,3072]{1,0:T(8,128)(2,1)S(1)}, bf16[1024,3072]{1,0:T(8,128)(2,1)}, u32[]{:S(2)}) copy-start(bf16[1024,3072]{1,0:T(8,128)(2,1)} %all-gather.2.cloned.1.call-done.weight_ref) | copy-start | bytes 18874372
  112.7 5.9 %copy-start.8 = (bf16[3072,64]{0,1:T(8,128)(2,1)S(1)}, bf16[3072,64]{0,1:T(8,128)(2,1)}, u32[]{:S(2)}) copy-start(bf16[3072,64]{0,1:T(8,128)(2,1)} %param.25) | copy-start | bytes 1179652
  112.7 10.1 %copy-start.1 = (bf16[2,1,1,24,3072]{4,3,2,1,0:T(8,128)(2,1)S(1)}, bf16[2,1,1,24,3072]{4,3,2,1,0:T(8,128)(2,1)}, u32[]{:S(2)}) copy-start(bf16[2,1,1,24,3072]{4,3,2,1,0:T(8,128)(2,1)} %param.16) | copy-start | bytes 884740
  112.7 10.1 %copy-start.2 = (bf16[1,1,24,3072]{3,2,1,0:T(8,128)(2,1)S(1)}, bf16[1,1,24,3072]{3,2,1,0:T(8,128)(2,1)}, u32[]{:S(2)}) copy-start(bf16[1,1,24,3072]{3,2,1,0:T(8,128)(2,1)} %param.15) | copy-start | bytes 442372
  112.7 10.1 %copy-start.3 = (f32[3072]{0:T(1024)S(1)}, f32[3072]{0:T(1024)}, u32[]{:S(2)}) copy-start(f32[3072]{0:T(1024)} %param.21) | copy-start | bytes 36868
  112.7 10.1 %copy-start.4 = (f32[3072]{0:T(1024)S(1)}, f32[3072]{0:T(1024)}, u32[]{:S(2)}) copy-start(f32[3072]{0:T(1024)} %param.22) | copy-start | bytes 36868
  112.7 10.1 %copy-start.5 = (f32[3072]{0:T(1024)S(1)}, f32[3072]{0:T(1024)}, u32[]{:S(2)}) copy-start(f32[3072]{0:T(1024)} %param.23) | copy-start | bytes 36868
  112.7 10.1 %copy-start.6 = (s32[2,1,1,24]{3,2,1,0:T(1,128)S(1)}, s32[2,1,1,24]{3,2,1,0:T(1,128)}, u32[]{:S(2)}) copy-start(s32[2,1,1,24]{3,2,1,0:T(1,128)} %param.17) | copy-start | bytes 580
  112.8 10.0 %copy-start.7 = (f32[64]{0:T(128)S(1)}, f32[64]{0:T(128)}, u32[]{:S(2)}) copy-start(f32[64]{0:T(128)} %param.26) | copy-start | bytes 772
  115.4 7.4 %collective-permute-start = (bf16[24,3072]{1,0:T(8,128)(2,1)S(1)}, bf16[24,3072]{1,0:T(8,128)(2,1)S(1)}, u32[]{:S(2)}, u32[]{:S(2)}) collective-permute-start(bf16[24,3072]{1,0:T(8,128)(2,1)S(1)} %get-tuple-element.7), channel_id=1, source_target_pairs={{0,256},{256,0},{1,257},{257,1},{2,258},{258,2},{3,259},{259,3},{4... | collective-permute-start | bytes 442376 | tf_op jit(solution)/shard_map/ppermute | solution.py:331
  122.8 19.4 %copy-start.9 = (f32[512]{0:T(512)S(1)}, f32[512]{0:T(512)}, u32[]{:S(2)}) copy-start(f32[512]{0:T(512)} %param.28) | copy-start | bytes 6148
  125.9 32.8 %all-to-all-start.4 = ((bf16[512,2,128]{2,1,0:T(2,128)(2,1)}), bf16[512,2,128]{2,1,0:T(2,128)(2,1)S(1)}, u32[]{:S(2)}, u32[]{:S(2)}) async-start(bf16[512,2,128]{2,1,0:T(2,128)(2,1)} %reshape.66), calls=%async_computation.4 | async-start | bytes 524288 | tf_op jit(solution)/shard_map/all_to_all | solution.py:344
Sparse Core Ops, SparseCore 0:
  10.1 83.3 all-gather.1

commit v2 on v1

v2 whole, which is shorter than its diff:
```python
import math

import jax
import jax.numpy as jnp
from jax import lax
from jax.experimental import pallas as pl
from jax.experimental.pallas import tpu as pltpu
from jax.sharding import Mesh, PartitionSpec as P

HD = 128
HEADS = 16
F32 = jnp.float32
BF16 = jnp.bfloat16
MIB = 1 << 20

TOK = 24
FRAMES = 16
PIX = 1024
KEYS = 768

VMEM = pl.BlockSpec(memory_space=pltpu.VMEM)
SMEM = pl.BlockSpec(memory_space=pltpu.SMEM)

GRP = ("h", "z")
COL = ("ya", "yb", "l", "c")


def dot(a, b, contract):
    return lax.dot_general(a, b, ((contract[0], contract[1]), ((), ())), preferred_element_type=F32)


def pack_kernel(c_ref, q_ref, k_ref, v_ref, weight_ref, out_ref, half_ref):
    half = half_ref.shape[1]
    half_ref[...] = weight_ref[:, pl.ds(pl.multiple_of(c_ref[0] * half, 128), half)]
    for g in range(HEADS):
        cols = slice(g * HD, (g + 1) * HD)
        out_ref[g, :, 0:HD] = q_ref[:, cols]
        out_ref[g, :, HD : 2 * HD] = k_ref[:, cols]
        out_ref[g, :, 2 * HD : 3 * HD] = v_ref[:, cols]


def pack(c, q, k, v, weight):
    return pl.pallas_call(
        pack_kernel,
        out_shape=(
            jax.ShapeDtypeStruct((HEADS, TOK, 3 * HD), BF16),
            jax.ShapeDtypeStruct((weight.shape[0], weight.shape[1] // 2), BF16),
        ),
        in_specs=[SMEM] + [VMEM] * 4,
        out_specs=(VMEM, VMEM),
    )(c, q, k, v, weight)


def attend_kernel(q_ref, kv0_ref, kv1_ref, out_ref):
    scale = math.log2(math.e) / math.sqrt(HD)
    half = kv0_ref.shape[0]
    token = lax.broadcasted_iota(jnp.int32, (2 * TOK, HD), 0)
    lane = lax.broadcasted_iota(jnp.int32, (2 * TOK, HD), 1)
    base = lane - lax.rem(token, 3) * 3
    row = lax.broadcasted_iota(jnp.int32, (16, 2 * TOK), 0)
    spot = lax.broadcasted_iota(jnp.int32, (16, 2 * TOK), 1)
    pick = jnp.where(lax.div(spot, 3) == row, 1.0, 0.0).astype(BF16)
    runs = [(ref, slice(at, at + KEYS)) for ref in (kv0_ref, kv1_ref) for at in range(0, half, KEYS)]

    def column(i, carry):
        q = q_ref[i]

        def scores(n):
            ref, rows = runs[n]
            return dot(q, ref[rows, 0:HD], ((1,), (1,)))

        ahead = scores(0)
        top = total = o = None
        for n, (ref, rows) in enumerate(runs):
            s = ahead
            if n + 1 < len(runs):
                ahead = scores(n + 1)
            high = jnp.max(s, axis=1, keepdims=True) * scale
            if n:
                before = top
                top = jnp.maximum(before, high)
                shrink = jnp.exp2(before - top)
            else:
                top = high
            p = jnp.exp2(s * scale - top)
            here = jnp.sum(p, axis=1, keepdims=True)
            part = dot(p.astype(BF16), ref[rows, HD : 2 * HD], ((1,), (0,)))
            total = total * shrink + here if n else here
            o = o * shrink + part if n else part
        o = (o / total).reshape(2, 8, TOK, HD)
        log = top + jnp.log2(total)
        hi = log.astype(BF16).astype(F32)
        mid = (log - hi).astype(BF16).astype(F32)
        lo = log - hi - mid
        hi, mid, lo = (x.reshape(2, 8, TOK, 1) for x in (hi, mid, lo))
        for z in range(8):
            piece = [jnp.concatenate([x[0, z], x[1, z]], axis=0) for x in (hi, mid, lo)]
            spread = jnp.where(
                base == 0,
                piece[0],
                jnp.where(base == 1, piece[1], jnp.where(base == 2, piece[2], 0.0)),
            )
            stats = dot(pick, spread.astype(BF16), ((1,), (0,)))
            out_ref[z, i] = jnp.concatenate([o[0, z], o[1, z], stats], axis=0).astype(BF16)
        return carry

    lax.fori_loop(0, 4, column, 0)


def attend(q, kvs):
    return pl.pallas_call(
        attend_kernel,
        out_shape=jax.ShapeDtypeStruct((8, 4, 64, HD), BF16),
        in_specs=[VMEM] * 3,
        out_specs=VMEM,
        compiler_params=pltpu.CompilerParams(vmem_limit_bytes=32 * MIB),
    )(q, *kvs)


def hold_kernel(own_ref, out_ref, sem):
    copy = pltpu.make_async_copy(own_ref, out_ref, sem)
    copy.start()
    copy.wait()


def hold(own):
    return pl.pallas_call(
        hold_kernel,
        out_shape=jax.ShapeDtypeStruct(own.shape, BF16),
        in_specs=[pl.BlockSpec(memory_space=pltpu.HBM)],
        out_specs=VMEM,
        scratch_shapes=[pltpu.SemaphoreType.DMA],
        cost_estimate=pl.CostEstimate(flops=0, bytes_accessed=2 * own.size * 2, transcendentals=0),
        compiler_params=pltpu.CompilerParams(vmem_limit_bytes=8 * MIB),
    )(own)


def project_kernel(h_ref, c_ref, parts_ref, own_ref, other_ref, keep_ref, send_ref, att_ref, sum_ref):
    step = pl.program_id(0)

    @pl.when(step == 0)
    def join():
        join_parts(parts_ref, att_ref)

    @pl.when(step < 2)
    def near():
        sum_ref[...] = dot(att_ref[...], own_ref[...], ((1,), (0,)))

    @pl.when(step >= 2)
    def far():
        sum_ref[...] = dot(att_ref[...], other_ref[...], ((1,), (0,)))

    h = h_ref[0]
    keep_ref[...] = sum_ref[pl.ds(pl.multiple_of(h * TOK, 8), TOK), :]
    send_ref[...] = sum_ref[pl.ds(pl.multiple_of((1 - h) * TOK, 8), TOK), :].astype(BF16)


def join_parts(parts_ref, att_ref):
    token = lax.broadcasted_iota(jnp.int32, (2 * TOK, HD), 0)
    lane = lax.broadcasted_iota(jnp.int32, (2 * TOK, HD), 1)
    base = lane - lax.rem(token, 3) * 3
    mine = (base >= 0) & (base < 3)
    spot = lax.broadcasted_iota(jnp.int32, (2 * TOK, 16), 0)
    row = lax.broadcasted_iota(jnp.int32, (2 * TOK, 16), 1)
    pick = jnp.where(lax.div(spot, 3) == row, 1.0, 0.0).astype(BF16)
    for z in range(8):
        logs = []
        for j in range(4):
            spread = dot(pick, parts_ref[z, j, 48:64, :], ((1,), (0,)))
            logs.append(jnp.sum(jnp.where(mine, spread, 0.0), axis=1, keepdims=True))
        top = jnp.maximum(jnp.maximum(logs[0], logs[1]), jnp.maximum(logs[2], logs[3]))
        shares = [jnp.exp2(x - top) for x in logs]
        total = (shares[0] + shares[1]) + (shares[2] + shares[3])
        att = jnp.zeros((2 * TOK, HD), F32)
        for j in range(4):
            att = att + parts_ref[z, j, 0:48, :].astype(F32) * (shares[j] / total)
        att_ref[:, z * HD : (z + 1) * HD] = att.astype(BF16)


def project(h, c, parts, own, other):
    depth, half = own.shape
    block = half // 2

    def place(i, h_ref, c_ref):
        side = jnp.where(i < 2, c_ref[0], 1 - c_ref[0])
        return 0, side * 2 + lax.rem(i, 2)

    return pl.pallas_call(
        project_kernel,
        out_shape=(
            jax.ShapeDtypeStruct((TOK, 2 * half), F32),
            jax.ShapeDtypeStruct((TOK, 2 * half), BF16),
        ),
        grid_spec=pltpu.PrefetchScalarGridSpec(
            num_scalar_prefetch=2,
            grid=(4,),
            in_specs=[
                pl.BlockSpec(parts.shape, lambda i, h_ref, c_ref: (0, 0, 0, 0)),
                pl.BlockSpec((depth, block), lambda i, h_ref, c_ref: (0, jnp.minimum(i, 1))),
                pl.BlockSpec((depth, block), lambda i, h_ref, c_ref: (0, jnp.maximum(i - 2, 0))),
            ],
            out_specs=(pl.BlockSpec((TOK, block), place), pl.BlockSpec((TOK, block), place)),
            scratch_shapes=[
                pltpu.VMEM((2 * TOK, depth), BF16),
                pltpu.VMEM((2 * TOK, block), F32),
            ],
        ),
        compiler_params=pltpu.CompilerParams(vmem_limit_bytes=24 * MIB),
    )(h, c, parts, own, other)


def norm_kernel(
    h_ref, keep_ref, recv_ref, res_ref, cached_ref, use_ref, gate_ref, shift_ref, scale_ref, fw_ref, fb_ref,
    stream_ref, out_ref,
):
    eye = lax.broadcasted_iota(jnp.int32, (TOK, TOK), 0) == lax.broadcasted_iota(
        jnp.int32, (TOK, TOK), 1
    )
    mixed = res_ref[...].astype(F32)
    for b in range(2):
        used = use_ref[b : b + 1, :].astype(F32)
        column = jnp.sum(jnp.where(eye, used, 0.0), axis=1, keepdims=True)
        mixed = mixed + column * cached_ref[b].astype(F32)
    projected = keep_ref[...] + recv_ref[1 - h_ref[0]].astype(F32)
    stream = (mixed + gate_ref[...] * projected).astype(BF16)
    stream_ref[...] = stream
    x = stream.astype(F32)
    center = jnp.mean(x, axis=1, keepdims=True)
    off = x - center
    spread = jnp.mean(off * off, axis=1, keepdims=True)
    modulated = off * lax.rsqrt(spread + 1e-6) * (1.0 + scale_ref[...]) + shift_ref[...]
    latent = dot(modulated.astype(BF16), fw_ref[...], ((1,), (1,))) + fb_ref[...]
    latent = latent.astype(BF16)
    source = lax.broadcasted_iota(jnp.int32, (64, 64), 0)
    target = lax.broadcasted_iota(jnp.int32, (64, 64), 1)
    group = lax.div(target, 16)
    wanted = (lax.rem(group, 2) * 2 + lax.div(group, 2)) * 16 + lax.rem(target, 16)
    latent = dot(latent, jnp.where(source == wanted, 1.0, 0.0).astype(BF16), ((1,), (0,)))
    latent = latent.astype(BF16)
    band = lax.broadcasted_iota(jnp.int32, (FRAMES, TOK), 0)
    source = lax.broadcasted_iota(jnp.int32, (FRAMES, TOK), 1)
    first = lax.div(3 * band, 2) - 1
    pieces = [
        dot(jnp.where(source == first + k, 1.0, 0.0).astype(BF16), latent, ((1,), (0,)))
        for k in range(4)
    ]
    window = [x[:, 0:32] for x in pieces] + [x[:, 32:64] for x in pieces]
    window = jnp.concatenate(window, axis=1).reshape(FRAMES, 1, 2, HD)
    out_ref[...] = jnp.broadcast_to(window, (FRAMES, 32, 2, HD)).astype(BF16)


def norm(h, keep, recv, res, cached, use, gate, shift, scale, fw, fb):
    return pl.pallas_call(
        norm_kernel,
        out_shape=(
            jax.ShapeDtypeStruct(res.shape, BF16),
            jax.ShapeDtypeStruct((FRAMES, 32, 2, HD), BF16),
        ),
        in_specs=[SMEM] + [VMEM] * 10,
        out_specs=(VMEM, VMEM),
        compiler_params=pltpu.CompilerParams(vmem_limit_bytes=32 * MIB),
    )(h, keep, recv, res, cached, use, gate, shift, scale, fw, fb)


def frames_back(x, count, lane):
    if count == 0:
        return x
    moved = pltpu.roll(x, 64 * count, 1)
    start = x[:, 0:128]
    start = jnp.where(lane[:, 0:128] < 64, start, pltpu.roll(start, 64, 1))
    width = 128
    head = jnp.where(lane[:, 0:width] < 64 * count, start, moved[:, 0:width])
    return jnp.concatenate([head, moved[:, width:]], axis=1)


def column_shift(x, by, place):
    if by == 0:
        return x
    moved = pltpu.roll(x, (-by) % PIX, 1)
    edge = 63 if by == 1 else 0
    return jnp.where(place == edge, 0.0, moved)


def ready_kernel(w1_ref, w2_ref, out_ref):
    taps = w2_ref.shape[0]
    out_ref[0:taps, :] = w2_ref[...]
    out_ref[taps:, 0:taps] = jnp.transpose(w1_ref[...].astype(F32)).astype(BF16)


def ready(w1, w2):
    return pl.pallas_call(
        ready_kernel,
        out_shape=jax.ShapeDtypeStruct((432 + 512, 512), BF16),
        in_specs=[VMEM] * 2,
        out_specs=VMEM,
        cost_estimate=pl.CostEstimate(flops=0, bytes_accessed=1 << 23, transcendentals=0),
        compiler_params=pltpu.CompilerParams(vmem_limit_bytes=8 * MIB),
    )(w1, w2)


def conv_kernel(band_ref, own_ref, lat_ref, weights_ref, b1_ref, out_ref, taps_ref, first_ref, acc_ref):
    band = band_ref[0]
    lanes = own_ref[0]
    bias = jnp.transpose(jnp.broadcast_to(b1_ref[...], (8, 512)))[:, 0:1]
    lane16 = lax.broadcasted_iota(jnp.int32, (16, PIX), 1)
    place16 = lax.rem(lane16, 64)
    latent = jnp.transpose(lat_ref[...].astype(F32).reshape(PIX, 128))
    for r in range(8):
        row = latent[r * 16 : r * 16 + 16]
        for b in range(3):
            moved = column_shift(row, b - 1, place16)
            for t in range(3):
                at = r * 48 + b * 16
                taps_ref[t, at : at + 16, :] = frames_back(moved, 2 - t, lane16).astype(BF16)
    acc_ref[...] = jnp.zeros_like(acc_ref)
    odd = lax.rem(band, 2)
    for r in range(5):
        at = pl.multiple_of((odd + r) * 48, 16)
        patches = jnp.concatenate([taps_ref[t, pl.ds(at, 144), :] for t in range(3)], axis=0)
        first = dot(weights_ref[432:, 0:432], patches, ((1,), (0,))) + bias
        height = 3 * band - 1 + r
        inside = jnp.where((height >= 0) & (height < 48), 1.0, 0.0)
        v = (first * inside).astype(BF16).astype(F32)
        if 1 <= r <= 3:
            first_ref[...] = v
            own = first_ref[pl.ds(pl.multiple_of(lanes * 16, 16), 16), :]
            acc_ref[r - 1, 2, 16:32, :] += own
        half = 0.5 * v
        act = (half * jnp.tanh(half) + half).astype(BF16)
        z = dot(weights_ref[0:432, :], act, ((1,), (0,)))
        for a in range(3):
            o = r - a
            if 0 <= o < 3:
                for t in range(3):
                    acc_ref[o, t] += z[(t * 3 + a) * 48 : (t * 3 + a + 1) * 48]
    for o in range(3):
        total = None
        for t in range(3):
            u = acc_ref[o, t, 16:32, :]
            u = u + column_shift(acc_ref[o, t, 0:16, :], -1, place16)
            u = u + column_shift(acc_ref[o, t, 32:48, :], 1, place16)
            u = frames_back(u, 2 - t, lane16)
            total = u if total is None else total + u
        out_ref[o] = total.astype(BF16)


def conv(band, own, lat, weights, b1):
    return pl.pallas_call(
        conv_kernel,
        out_shape=jax.ShapeDtypeStruct((3, 16, PIX), BF16),
        in_specs=[SMEM] * 2 + [VMEM] * 3,
        out_specs=VMEM,
        scratch_shapes=[
            pltpu.VMEM((3, 8 * 48, PIX), BF16),
            pltpu.VMEM((512, PIX), F32),
            pltpu.VMEM((3, 3, 48, PIX), F32),
        ],
        compiler_params=pltpu.CompilerParams(vmem_limit_bytes=28 * MIB),
    )(band, own, lat, weights, b1)


def per_device(
    residual_in,
    cached,
    use_cached,
    queries,
    attn_keys,
    values,
    gate_mod,
    shift_mod,
    scale_mod,
    out_weight,
    final_weight,
    final_bias,
    first_weight,
    first_bias,
    second_weight,
):
    model_width = residual_in.shape[-1]
    channels = first_weight.shape[-1]
    h = lax.axis_index("h").astype(jnp.int32).reshape(1)
    c = lax.axis_index("c").astype(jnp.int32).reshape(1)
    tokens = (x.reshape(TOK, HEADS * HD) for x in (queries, attn_keys, values))
    packed, mine = pack(c, *tokens, out_weight)
    mine = lax.all_gather(mine, "z", axis=0, tiled=True)
    moved = lax.all_to_all(packed, GRP, split_axis=0, concat_axis=0, tiled=True)
    moved = moved.reshape(FRAMES * TOK, 3 * HD)
    kv = jnp.broadcast_to(moved[None, :, HD:], (4, FRAMES * TOK, 2 * HD))
    kv = lax.all_to_all(kv, "ya", split_axis=0, concat_axis=0, tiled=True)
    kv = kv.reshape(4 * FRAMES * TOK, 2 * HD)
    kvs = [kv, lax.ppermute(kv, "c", [(0, 1), (1, 0)])]
    q = jnp.broadcast_to(moved[None, :, :HD], (4, FRAMES * TOK, HD))
    q = lax.all_to_all(q, ("yb", "l"), split_axis=0, concat_axis=0, tiled=True)
    parts = attend(q, kvs)
    parts, mine = lax.optimization_barrier((parts, mine))
    theirs = lax.ppermute(mine, "c", [(0, 1), (1, 0)])
    mine = hold(mine)
    parts = lax.all_to_all(
        parts.reshape(32, 64, HD), ("z", "yb", "l"), split_axis=0, concat_axis=0, tiled=True
    )
    keep, send = project(h, c, parts.reshape(8, 4, 64, HD), mine, theirs)
    recv = lax.all_gather(send, "h", axis=0)
    stream, windows = norm(
        h,
        keep,
        recv,
        residual_in.reshape(TOK, model_width),
        cached.reshape(2, TOK, model_width),
        use_cached.reshape(2, TOK),
        gate_mod[None, :],
        shift_mod[None, :],
        scale_mod[None, :],
        final_weight.T,
        final_bias[None, :],
    )
    windows, w1, w2 = lax.optimization_barrier((windows, first_weight, second_weight))
    lat = lax.all_to_all(
        windows.reshape(512, 2, HD), GRP + COL, split_axis=0, concat_axis=0, tiled=True
    )
    band = lax.axis_index(GRP).astype(jnp.int32).reshape(1)
    own = lax.axis_index(COL).astype(jnp.int32).reshape(1)
    w2 = jnp.transpose(w2, (1, 2, 3, 0, 4)).reshape(27 * 16, channels)
    weights = ready(w1.reshape(27 * 16, channels), w2)
    out = conv(band, own, lat, weights, first_bias[None, :])
    return stream.reshape(residual_in.shape), jnp.transpose(out, (1, 0, 2))


def solution(mesh):
    fine = Mesh(mesh.devices.reshape(2, 8, 4, 2, 2, 2), GRP + COL)
    return jax.shard_map(
        per_device,
        mesh=fine,
        in_specs=(
            P(GRP, COL, None, None),
            P(None, GRP, COL, None, None),
            P(None, GRP, COL, None),
            P(GRP, COL, None, None),
            P(GRP, COL, None, None),
            P(GRP, COL, None, None),
            P(),
            P(),
            P(),
            P(GRP, None),
            P(),
            P(),
            P(),
            P(),
            P(COL, None, None, None, None),
        ),
        out_specs=(P(GRP, COL, None, None), P(COL, GRP, None)),
        check_vma=False,
    )
```

time: 176 us -> 163 us (0.926)
  blocking collectives: 51.2 us -> 66.4 us
  waiting for transfers between devices: 43.2 us -> 28.2 us
  starting transfers between devices: 33.3 us -> 25 us
  local copies, waits for them, and re-layouts: 7.19 us -> 4.08 us
    all_to_all x3 -> x2, starting transfers between devices: 30 us -> 17.2 us  [the longest x1 11.6 us: per_device(): lax.all_to_all(windows.reshape(512, 2, HD), GRP + COL, split_axis=0, conc...]
    all_to_all x3 -> x2, waiting for transfers between devices: 38.8 us -> 28.2 us  [the longest x1 14.3 us: per_device(): lax.all_to_all(windows.reshape(512, 2, HD), GRP + COL, split_axis=0, conc...]
    all_to_all x1 -> x2, blocking collectives: 27.1 us -> 36.1 us  [the longest x1 27.1 us: per_device(): kv = lax.all_to_all(kv, 'ya', split_axis=0, concat_axis=0, tiled=True)]
    all_gather x0 -> x1, blocking collectives: none -> 6.17 us  [per_device(): recv = lax.all_gather(send, 'h', axis=0)]
    ppermute x1 -> x2, starting transfers between devices: 3.23 us -> 7.71 us  [the longest x1 4.38 us: per_device(): kvs = [kv, lax.ppermute(kv, 'c', [(0, 1), (1, 0)])]]
    ppermute x1 -> x2, waiting for transfers between devices: 3.76 us -> 0.01 us  [the longest x1 0.01 us: per_device(): kvs = [kv, lax.ppermute(kv, 'c', [(0, 1), (1, 0)])]]
    pallas_call x3 -> x5, Pallas kernels: 15 us -> 16 us  [the longest x1 8.32 us: attend(): pl.pallas_call(attend_kernel, out_shape=jax.ShapeDtypeStruct((8, 4, 64, H...]
  transfers between devices with their start and end apart: 5 -> 5, of which waited for: 4 -> 2; matrix products, arithmetic and copies ran while one was open for 2% -> 0% of each run, Pallas kernels for 7% -> 5%
where the time goes in v2:
time: 163 us
  blocking collectives  66.4 us (41%)
  waiting for transfers between devices  28.2 us (17%)
  starting transfers between devices  25 us (15%)
  Pallas kernels  24.8 us (15%)
  between operations  14.3 us (9%)
  local copies, waits for them, and re-layouts  4.08 us (3%)
    all_to_all x1, blocking collectives, per_device(): kv = lax.all_to_all(kv, 'ya', split_axis=0, concat_axis=0, tiled=True)  27.1 us
    all_to_all x1, blocking collectives, per_device(): moved = lax.all_to_all(packed, GRP, split_axis=0, concat_axis=0, tiled=True)  24.1 us
    all_to_all x1, waiting for transfers between devices, per_device(): lax.all_to_all(windows.reshape(512, 2, HD), GRP + COL, split_axis=0, conc...  14.3 us
    all_to_all x1, waiting for transfers between devices, per_device(): lax.all_to_all(parts.reshape(32, 64, HD), ('z', 'yb', 'l'), split_axis=0,...  13.9 us
    all_to_all x1, starting transfers between devices, per_device(): lax.all_to_all(windows.reshape(512, 2, HD), GRP + COL, split_axis=0, conc...  11.6 us
    all_to_all x1, blocking collectives, per_device(): q = lax.all_to_all(q, ('yb', 'l'), split_axis=0, concat_axis=0, tiled=True)  9.03 us
    pallas_call x1, Pallas kernels, attend(): pl.pallas_call(attend_kernel, out_shape=jax.ShapeDtypeStruct((8, 4, 64, H...  8.32 us
    pallas_call x1, Pallas kernels, conv(): pl.pallas_call(conv_kernel, out_shape=jax.ShapeDtypeStruct((3, 16, PIX),...  7.03 us
  transfers between devices with their start and end apart: 5, of which 2 were waited for; matrix products, arithmetic and copies ran while one was open for 0% of the time, Pallas kernels for 5%

profile of v2, /device:TPU:1, one launch (start us, length us, event | category | flops | bytes accessed | tf_op | source)
XLA Modules:
  0.0 162.6 jit_solution(2277092757002778962)
XLA Ops:
  7.2 0.0 all-gather.3.cloned.1.call-start
  7.2 2.2 %shard_map.158 = (bf16[16,24,384]{2,1,0:T(8,128)(2,1)}, bf16[128,1536]{1,0:T(8,128)(2,1)}) custom-call(s32[1]{0:T(128)} %bitcast.1.c_ref, bf16[24,2048]{1,0:T(8,128)(2,1)} %bitcast.45, bf16[24,2048]{1,0:T(8,128)(2,1)} %bitcast.46, bf16[24,2048]{1,0:T(8,128)(2,1)} %bitcast.47, bf16[128,3072]{1,0:T(8,128)(2,1)} %weight_ref.1), custom_call_target="tpu_custom_call" | custom-call | tf_op jit(solution)/shard_map/pallas_call | solution.py:43
  9.4 0.0 all-gather.3.cloned.1.call-update
  9.5 24.1 %all_to_all.25 = bf16[16,24,384]{2,1,0:T(8,128)(2,1)S(1)} all-to-all(bf16[16,24,384]{2,1,0:T(8,128)(2,1)} %get-tuple-element.13), channel_id=1, replica_groups=mesh['h'=2,'z'=8,'ya'=4,'yb'=2,'l'=2,'c'=2] {'h','z'}, dimensions={0} | all-to-all | bytes 589824 | tf_op jit(solution)/shard_map/all_to_all | solution.py:386
  33.6 0.1 broadcast_in_dim.28
  33.6 27.1 %all_to_all.26 = bf16[4,384,256]{2,1,0:T(8,128)(2,1)S(1)} all-to-all(bf16[4,384,256]{2,1,0:T(8,128)(2,1)S(1)} %broadcast_in_dim.28), channel_id=1, replica_groups=mesh['h'=2,'z'=8,'ya'=4,'yb'=2,'l'=2,'c'=2] {'ya'}, dimensions={0} | all-to-all | bytes 1572864 | tf_op jit(solution)/shard_map/all_to_all | solution.py:389
  60.7 4.4 %collective-permute-start = (bf16[1536,256]{1,0:T(8,128)(2,1)S(1)}, bf16[1536,256]{1,0:T(8,128)(2,1)S(1)}, u32[]{:S(2)}, u32[]{:S(2)}) collective-permute-start(bf16[1536,256]{1,0:T(8,128)(2,1)S(1)} %bitcast.28), channel_id=1, source_target_pairs={{0,1},{1,0},{2,3},{3,2},{4,5},{5,4},{6,7},{7,6},{8,9},{9,8},{10,11... | collective-permute-start | bytes 2359304 | tf_op jit(solution)/shard_map/ppermute | solution.py:391
  65.1 0.1 broadcast_in_dim.27
  65.2 9.0 %all_to_all.27.q_ref = bf16[4,384,128]{2,1,0:T(8,128)(2,1)S(1)} all-to-all(bf16[4,384,128]{2,1,0:T(8,128)(2,1)S(1)} %broadcast_in_dim.27), channel_id=1, replica_groups=mesh['h'=2,'z'=8,'ya'=4,'yb'=2,'l'=2,'c'=2] {'yb','l'}, dimensions={0} | all-to-all | bytes 786432 | tf_op jit(solution)/shard_map/all_to_all | solution.py:393
  74.2 0.0 collective-permute-done.kv1_ref
  74.2 8.3 %shard_map.159 = bf16[8,4,64,128]{3,2,1,0:T(8,128)(2,1)} custom-call(bf16[4,384,128]{2,1,0:T(8,128)(2,1)S(1)} %all_to_all.27.q_ref, bf16[1536,256]{1,0:T(8,128)(2,1)S(1)} %bitcast.29, bf16[1536,256]{1,0:T(8,128)(2,1)S(1)} %collective-permute-done.kv1_ref), custom_call_target="tpu_custom_call" | custom-call | tf_op jit(solution)/shard_map/pallas_call | solution.py:111
  82.5 0.0 all-gather.3.cloned.1.call-done.own_ref
  82.5 3.3 %collective-permute-start.1 = (bf16[1024,1536]{1,0:T(8,128)(2,1)}, bf16[1024,1536]{1,0:T(8,128)(2,1)}, u32[]{:S(2)}, u32[]{:S(2)}) collective-permute-start(bf16[1024,1536]{1,0:T(8,128)(2,1)} %all-gather.3.cloned.1.call-done.own_ref), channel_id=1, source_target_pairs={{0,1},{1,0},{2,3},{3,2},{4,5},{5,4},{6,7},{7,6},{8,9},{9,8},{10,11... | collective-permute-start | bytes 9437192 | tf_op jit(solution)/shard_map/ppermute | solution.py:396
  85.8 5.6 %all-to-all-start.3 = ((bf16[32,64,128]{2,1,0:T(8,128)(2,1)}), bf16[32,64,128]{2,1,0:T(8,128)(2,1)}, u32[]{:S(2)}, u32[]{:S(2)}) async-start(bf16[32,64,128]{2,1,0:T(8,128)(2,1)} %bitcast.7), calls=%async_computation.3 | async-start | bytes 1048576 | tf_op jit(solution)/shard_map/all_to_all | solution.py:398
  91.5 0.0 copy-start
  91.5 1.9 %copy-done = bf16[1024,1536]{1,0:T(8,128)(2,1)S(1)} copy-done((bf16[1024,1536]{1,0:T(8,128)(2,1)S(1)}, bf16[1024,1536]{1,0:T(8,128)(2,1)}, u32[]{:S(2)}) %copy-start) | copy-done | bytes 3145752
  93.4 0.2 shard_map.160.own_ref
  93.6 13.9 %all-to-all-done.3 = bf16[32,64,128]{2,1,0:T(8,128)(2,1)} async-done(((bf16[32,64,128]{2,1,0:T(8,128)(2,1)}), bf16[32,64,128]{2,1,0:T(8,128)(2,1)}, u32[]{:S(2)}, u32[]{:S(2)}) %all-to-all-start.3) | async-done | bytes 524320 | tf_op jit(solution)/shard_map/all_to_all | solution.py:398
  107.5 0.0 collective-permute-done.1.other_ref
  107.5 0.0 copy-start.3
  107.5 0.0 copy-start.4
  107.5 0.0 copy-start.5
  107.5 0.0 copy-start.6
  107.5 0.0 copy-start.7
  107.5 0.0 copy-start.8
  107.6 0.0 copy-start.10
  107.6 0.0 copy-start.11
  107.6 5.0 %shard_map.161 = (f32[24,3072]{1,0:T(8,128)S(1)}, bf16[24,3072]{1,0:T(8,128)(2,1)S(1)}) custom-call(s32[1]{0:T(128)} %bitcast.h_ref, s32[1]{0:T(128)} %bitcast.1.c_ref, bf16[8,4,64,128]{3,2,1,0:T(8,128)(2,1)} %bitcast.8.parts_ref, bf16[1024,1536]{1,0:T(8,128)(2,1)S(1)} %shard_map.160.own_ref, bf16[1024,1536]{1,0:T(8,128)(2,1)} %collective-permute-done.1.other_ref), custom_call_target="tpu_custom_call" | custom-call | tf_op jit(solution)/shard_map/pallas_call | solution.py:188
  112.6 0.0 copy-start.9
  112.6 6.2 %all-gather = bf16[48,3072]{1,0:T(8,128)(2,1)S(1)} all-gather(bf16[24,3072]{1,0:T(8,128)(2,1)S(1)} %get-tuple-element.18), channel_id=2, replica_groups=mesh['h'=2,'z'=8,'ya'=4,'yb'=2,'l'=2,'c'=2] {'h'}, dimensions={0}, use_global_device_ids=true | all-gather | bytes 442368 | tf_op jit(solution)/shard_map/all_gather | solution.py:402
  118.8 0.0 copy-done.3
  118.8 0.0 copy-done.4
  118.8 0.0 copy-done.5
  118.8 0.0 copy-done.6
  118.8 0.0 copy-done.7
  118.8 0.0 copy-done.8
  118.8 0.0 copy-done.10
  118.8 0.0 copy-done.11
  118.9 1.8 %shard_map.162 = (bf16[24,3072]{1,0:T(8,128)(2,1)}, bf16[16,32,2,128]{3,2,1,0:T(2,128)(2,1)}) custom-call(s32[1]{0:T(128)} %bitcast.h_ref, f32[24,3072]{1,0:T(8,128)S(1)} %get-tuple-element.17.keep_ref, bf16[2,24,3072]{2,1,0:T(8,128)(2,1)S(1)} %bitcast.30, bf16[24,3072]{1,0:T(8,128)(2,1)S(1)} %bitcast.35, bf16[2,24,3072]{2,1,0:T(8,128)(2,1)S(1)} %bitcast.34, ...), custom_call_target="tpu_custom_call" | custom-call | tf_op jit(solution)/shard_map/pallas_call | solution.py:253
  120.6 11.6 %all-to-all-start.4 = ((bf16[512,2,128]{2,1,0:T(2,128)(2,1)}), bf16[512,2,128]{2,1,0:T(2,128)(2,1)S(1)}, u32[]{:S(2)}, u32[]{:S(2)}) async-start(bf16[512,2,128]{2,1,0:T(2,128)(2,1)} %bitcast.21), calls=%async_computation.4 | async-start | bytes 524288 | tf_op jit(solution)/shard_map/all_to_all | solution.py:417
  132.3 0.0 copy-start.1
  132.3 1.0 copy-done.1
  133.3 0.0 copy-start.2
  133.3 1.0 copy-done.2
  134.3 0.2 shard_map.163.weights_ref
  134.5 14.3 %all-to-all-done.4.lat_ref = bf16[512,2,128]{2,1,0:T(2,128)(2,1)S(1)} async-done(((bf16[512,2,128]{2,1,0:T(2,128)(2,1)}), bf16[512,2,128]{2,1,0:T(2,128)(2,1)S(1)}, u32[]{:S(2)}, u32[]{:S(2)}) %all-to-all-start.4) | async-done | bytes 262176 | tf_op jit(solution)/shard_map/all_to_all | solution.py:417
  148.8 0.0 copy-done.9
  148.8 7.0 %shard_map.164 = bf16[3,16,1024]{2,1,0:T(8,128)(2,1)} custom-call(s32[1]{0:T(128)} %bitcast.19.band_ref, s32[1]{0:T(128)} %bitcast.20.own_ref, bf16[512,2,128]{2,1,0:T(2,128)(2,1)S(1)} %all-to-all-done.4.lat_ref, bf16[944,512]{1,0:T(8,128)(2,1)S(1)} %shard_map.163.weights_ref, f32[1,512]{1,0:T(1,128)S(1)} %bitcast.39), custom_call_target="tpu_custom_call" | custom-call | tf_op jit(solution)/shard_map/pallas_call | solution.py:348
  (2 shorter events, 0.0 us)
Async XLA Ops:
  7.2 75.3 %all-gather.3.cloned.1.call-start = ((), (), s32[]{:S(2)}) async-start(), calls=%async_computation.5 | async-start | bytes 3538944 | tf_op jit(solution)/shard_map/all_gather | solution.py:385
  60.7 13.5 %collective-permute-start = (bf16[1536,256]{1,0:T(8,128)(2,1)S(1)}, bf16[1536,256]{1,0:T(8,128)(2,1)S(1)}, u32[]{:S(2)}, u32[]{:S(2)}) collective-permute-start(bf16[1536,256]{1,0:T(8,128)(2,1)S(1)} %bitcast.28), channel_id=1, source_target_pairs={{0,1},{1,0},{2,3},{3,2},{4,5},{5,4},{6,7},{7,6},{8,9},{9,8},{10,11... | collective-permute-start | bytes 2359304 | tf_op jit(solution)/shard_map/ppermute | solution.py:391
  82.5 25.0 %collective-permute-start.1 = (bf16[1024,1536]{1,0:T(8,128)(2,1)}, bf16[1024,1536]{1,0:T(8,128)(2,1)}, u32[]{:S(2)}, u32[]{:S(2)}) collective-permute-start(bf16[1024,1536]{1,0:T(8,128)(2,1)} %all-gather.3.cloned.1.call-done.own_ref), channel_id=1, source_target_pairs={{0,1},{1,0},{2,3},{3,2},{4,5},{5,4},{6,7},{7,6},{8,9},{9,8},{10,11... | collective-permute-start | bytes 9437192 | tf_op jit(solution)/shard_map/ppermute | solution.py:396
  85.8 21.7 %all-to-all-start.3 = ((bf16[32,64,128]{2,1,0:T(8,128)(2,1)}), bf16[32,64,128]{2,1,0:T(8,128)(2,1)}, u32[]{:S(2)}, u32[]{:S(2)}) async-start(bf16[32,64,128]{2,1,0:T(8,128)(2,1)} %bitcast.7), calls=%async_computation.3 | async-start | bytes 1048576 | tf_op jit(solution)/shard_map/all_to_all | solution.py:398
  91.5 1.9 %copy-start = (bf16[1024,1536]{1,0:T(8,128)(2,1)S(1)}, bf16[1024,1536]{1,0:T(8,128)(2,1)}, u32[]{:S(2)}) copy-start(bf16[1024,1536]{1,0:T(8,128)(2,1)} %all-gather.3.cloned.1.call-done.own_ref) | copy-start | bytes 9437188
  107.5 11.3 %copy-start.3 = (bf16[3072,64]{0,1:T(8,128)(2,1)S(1)}, bf16[3072,64]{0,1:T(8,128)(2,1)}, u32[]{:S(2)}) copy-start(bf16[3072,64]{0,1:T(8,128)(2,1)} %param.25) | copy-start | bytes 1179652
  107.5 11.3 %copy-start.4 = (bf16[2,1,1,24,3072]{4,3,2,1,0:T(8,128)(2,1)S(1)}, bf16[2,1,1,24,3072]{4,3,2,1,0:T(8,128)(2,1)}, u32[]{:S(2)}) copy-start(bf16[2,1,1,24,3072]{4,3,2,1,0:T(8,128)(2,1)} %param.16) | copy-start | bytes 884740
  107.5 11.3 %copy-start.5 = (bf16[1,1,24,3072]{3,2,1,0:T(8,128)(2,1)S(1)}, bf16[1,1,24,3072]{3,2,1,0:T(8,128)(2,1)}, u32[]{:S(2)}) copy-start(bf16[1,1,24,3072]{3,2,1,0:T(8,128)(2,1)} %param.15) | copy-start | bytes 442372
  107.5 11.3 %copy-start.6 = (f32[3072]{0:T(1024)S(1)}, f32[3072]{0:T(1024)}, u32[]{:S(2)}) copy-start(f32[3072]{0:T(1024)} %param.21) | copy-start | bytes 36868
  107.5 11.3 %copy-start.7 = (f32[3072]{0:T(1024)S(1)}, f32[3072]{0:T(1024)}, u32[]{:S(2)}) copy-start(f32[3072]{0:T(1024)} %param.22) | copy-start | bytes 36868
  107.5 11.3 %copy-start.8 = (f32[3072]{0:T(1024)S(1)}, f32[3072]{0:T(1024)}, u32[]{:S(2)}) copy-start(f32[3072]{0:T(1024)} %param.23) | copy-start | bytes 36868
  107.6 11.3 %copy-start.10 = (s32[2,1,1,24]{3,2,1,0:T(1,128)S(1)}, s32[2,1,1,24]{3,2,1,0:T(1,128)}, u32[]{:S(2)}) copy-start(s32[2,1,1,24]{3,2,1,0:T(1,128)} %param.17) | copy-start | bytes 580
  107.6 11.3 %copy-start.11 = (f32[64]{0:T(128)S(1)}, f32[64]{0:T(128)}, u32[]{:S(2)}) copy-start(f32[64]{0:T(128)} %param.26) | copy-start | bytes 772
  112.6 36.2 %copy-start.9 = (f32[512]{0:T(512)S(1)}, f32[512]{0:T(512)}, u32[]{:S(2)}) copy-start(f32[512]{0:T(512)} %param.28) | copy-start | bytes 6148
  120.6 28.1 %all-to-all-start.4 = ((bf16[512,2,128]{2,1,0:T(2,128)(2,1)}), bf16[512,2,128]{2,1,0:T(2,128)(2,1)S(1)}, u32[]{:S(2)}, u32[]{:S(2)}) async-start(bf16[512,2,128]{2,1,0:T(2,128)(2,1)} %bitcast.21), calls=%async_computation.4 | async-start | bytes 524288 | tf_op jit(solution)/shard_map/all_to_all | solution.py:417
  132.3 1.0 copy-start.1
  133.3 1.0 copy-start.2
Sparse Core Ops, SparseCore 0:
  10.1 53.7 all-gather.2

commit v3 on v2

--- a/solution.py
+++ b/solution.py
@@ -56,10 +56,10 @@
     half = kv0_ref.shape[0]
     token = lax.broadcasted_iota(jnp.int32, (2 * TOK, HD), 0)
     lane = lax.broadcasted_iota(jnp.int32, (2 * TOK, HD), 1)
-    base = lane - lax.rem(token, 3) * 3
-    row = lax.broadcasted_iota(jnp.int32, (16, 2 * TOK), 0)
-    spot = lax.broadcasted_iota(jnp.int32, (16, 2 * TOK), 1)
-    pick = jnp.where(lax.div(spot, 3) == row, 1.0, 0.0).astype(BF16)
+    base = lane - lax.rem(token, 6) * 3
+    row = lax.broadcasted_iota(jnp.int32, (8, 2 * TOK), 0)
+    spot = lax.broadcasted_iota(jnp.int32, (8, 2 * TOK), 1)
+    pick = jnp.where(lax.div(spot, 6) == row, 1.0, 0.0).astype(BF16)
     runs = [(ref, slice(at, at + KEYS)) for ref in (kv0_ref, kv1_ref) for at in range(0, half, KEYS)]
 
     def column(i, carry):
@@ -110,7 +110,7 @@
 def attend(q, kvs):
     return pl.pallas_call(
         attend_kernel,
-        out_shape=jax.ShapeDtypeStruct((8, 4, 64, HD), BF16),
+        out_shape=jax.ShapeDtypeStruct((8, 4, 56, HD), BF16),
         in_specs=[VMEM] * 3,
         out_specs=VMEM,
         compiler_params=pltpu.CompilerParams(vmem_limit_bytes=32 * MIB),
@@ -158,22 +158,23 @@
 def join_parts(parts_ref, att_ref):
     token = lax.broadcasted_iota(jnp.int32, (2 * TOK, HD), 0)
     lane = lax.broadcasted_iota(jnp.int32, (2 * TOK, HD), 1)
-    base = lane - lax.rem(token, 3) * 3
+    base = lane - lax.rem(token, 6) * 3
     mine = (base >= 0) & (base < 3)
-    spot = lax.broadcasted_iota(jnp.int32, (2 * TOK, 16), 0)
-    row = lax.broadcasted_iota(jnp.int32, (2 * TOK, 16), 1)
-    pick = jnp.where(lax.div(spot, 3) == row, 1.0, 0.0).astype(BF16)
+    spot = lax.broadcasted_iota(jnp.int32, (2 * TOK, 8), 0)
+    row = lax.broadcasted_iota(jnp.int32, (2 * TOK, 8), 1)
+    pick = jnp.where(lax.div(spot, 6) == row, 1.0, 0.0).astype(BF16)
     for z in range(8):
         logs = []
+        pieces = [parts_ref[z, j].astype(F32) for j in range(4)]
         for j in range(4):
-            spread = dot(pick, parts_ref[z, j, 48:64, :], ((1,), (0,)))
+            spread = dot(pick, pieces[j][48:56].astype(BF16), ((1,), (0,)))
             logs.append(jnp.sum(jnp.where(mine, spread, 0.0), axis=1, keepdims=True))
         top = jnp.maximum(jnp.maximum(logs[0], logs[1]), jnp.maximum(logs[2], logs[3]))
         shares = [jnp.exp2(x - top) for x in logs]
         total = (shares[0] + shares[1]) + (shares[2] + shares[3])
         att = jnp.zeros((2 * TOK, HD), F32)
         for j in range(4):
-            att = att + parts_ref[z, j, 0:48, :].astype(F32) * (shares[j] / total)
+            att = att + pieces[j][0:48] * (shares[j] / total)
         att_ref[:, z * HD : (z + 1) * HD] = att.astype(BF16)
 
 
@@ -305,7 +306,8 @@
     lane16 = lax.broadcasted_iota(jnp.int32, (16, PIX), 1)
     place16 = lax.rem(lane16, 64)
     latent = jnp.transpose(lat_ref[...].astype(F32).reshape(PIX, 128))
-    for r in range(8):
+    latent = jnp.where(lax.rem(band, 2) == 1, latent[16:128], latent[0:112])
+    for r in range(7):
         row = latent[r * 16 : r * 16 + 16]
         for b in range(3):
             moved = column_shift(row, b - 1, place16)
@@ -313,34 +315,32 @@
                 at = r * 48 + b * 16
                 taps_ref[t, at : at + 16, :] = frames_back(moved, 2 - t, lane16).astype(BF16)
     acc_ref[...] = jnp.zeros_like(acc_ref)
-    odd = lax.rem(band, 2)
     for r in range(5):
-        at = pl.multiple_of((odd + r) * 48, 16)
-        patches = jnp.concatenate([taps_ref[t, pl.ds(at, 144), :] for t in range(3)], axis=0)
+        patches = jnp.concatenate([taps_ref[t, r * 48 : r * 48 + 144, :] for t in range(3)], axis=0)
         first = dot(weights_ref[432:, 0:432], patches, ((1,), (0,))) + bias
         height = 3 * band - 1 + r
         inside = jnp.where((height >= 0) & (height < 48), 1.0, 0.0)
-        v = (first * inside).astype(BF16).astype(F32)
+        rounded = (first * inside).astype(BF16)
+        v = rounded.astype(F32)
         if 1 <= r <= 3:
-            first_ref[...] = v
-            own = first_ref[pl.ds(pl.multiple_of(lanes * 16, 16), 16), :]
-            acc_ref[r - 1, 2, 16:32, :] += own
+            first_ref[r - 1] = rounded
         half = 0.5 * v
         act = (half * jnp.tanh(half) + half).astype(BF16)
-        z = dot(weights_ref[0:432, :], act, ((1,), (0,)))
-        for a in range(3):
-            o = r - a
-            if 0 <= o < 3:
-                for t in range(3):
-                    acc_ref[o, t] += z[(t * 3 + a) * 48 : (t * 3 + a + 1) * 48]
+        low, high = max(r - 2, 0), min(r, 2)
+        z = dot(weights_ref[low * 144 : (high + 1) * 144, :], act, ((1,), (0,)))
+        for a in range(low, high + 1):
+            for t in range(3):
+                at = ((a - low) * 3 + t) * 48
+                acc_ref[r - a, t] += z[at : at + 48]
     for o in range(3):
-        total = None
+        own = pl.ds(pl.multiple_of(lanes * 16, 16), 16)
+        total = first_ref[o, own, :].astype(F32)
         for t in range(3):
             u = acc_ref[o, t, 16:32, :]
             u = u + column_shift(acc_ref[o, t, 0:16, :], -1, place16)
             u = u + column_shift(acc_ref[o, t, 32:48, :], 1, place16)
             u = frames_back(u, 2 - t, lane16)
-            total = u if total is None else total + u
+            total = total + u
         out_ref[o] = total.astype(BF16)
 
 
@@ -351,8 +351,8 @@
         in_specs=[SMEM] * 2 + [VMEM] * 3,
         out_specs=VMEM,
         scratch_shapes=[
-            pltpu.VMEM((3, 8 * 48, PIX), BF16),
-            pltpu.VMEM((512, PIX), F32),
+            pltpu.VMEM((3, 7 * 48, PIX), BF16),
+            pltpu.VMEM((3, 512, PIX), BF16),
             pltpu.VMEM((3, 3, 48, PIX), F32),
         ],
         compiler_params=pltpu.CompilerParams(vmem_limit_bytes=28 * MIB),
@@ -396,9 +396,9 @@
     theirs = lax.ppermute(mine, "c", [(0, 1), (1, 0)])
     mine = hold(mine)
     parts = lax.all_to_all(
-        parts.reshape(32, 64, HD), ("z", "yb", "l"), split_axis=0, concat_axis=0, tiled=True
+        parts.reshape(32, 56, HD), ("z", "yb", "l"), split_axis=0, concat_axis=0, tiled=True
     )
-    keep, send = project(h, c, parts.reshape(8, 4, 64, HD), mine, theirs)
+    keep, send = project(h, c, parts.reshape(8, 4, 56, HD), mine, theirs)
     recv = lax.all_gather(send, "h", axis=0)
     stream, windows = norm(
         h,
@@ -419,7 +419,7 @@
     )
     band = lax.axis_index(GRP).astype(jnp.int32).reshape(1)
     own = lax.axis_index(COL).astype(jnp.int32).reshape(1)
-    w2 = jnp.transpose(w2, (1, 2, 3, 0, 4)).reshape(27 * 16, channels)
+    w2 = jnp.transpose(w2, (2, 1, 3, 0, 4)).reshape(27 * 16, channels)
     weights = ready(w1.reshape(27 * 16, channels), w2)
     out = conv(band, own, lat, weights, first_bias[None, :])
     return stream.reshape(residual_in.shape), jnp.transpose(out, (1, 0, 2))

time: 163 us -> 161 us (0.988)
    unnamed x24 -> x22, local copies, waits for them, and re-layouts: 3.95 us -> 1.94 us
  transfers between devices with their start and end apart: 5 -> 5, of which waited for: 2 -> 2; matrix products, arithmetic and copies ran while one was open for 0% -> 1% of each run, Pallas kernels for 5% -> 5%
where the time goes in v3:
time: 161 us
  blocking collectives  66.5 us (41%)
  waiting for transfers between devices  28 us (17%)
  starting transfers between devices  24.6 us (15%)
  Pallas kernels  24.4 us (15%)
  between operations  14.3 us (9%)
  local copies, waits for them, and re-layouts  3.11 us (2%)
    all_to_all x1, blocking collectives, per_device(): kv = lax.all_to_all(kv, 'ya', split_axis=0, concat_axis=0, tiled=True)  27.1 us
    all_to_all x1, blocking collectives, per_device(): moved = lax.all_to_all(packed, GRP, split_axis=0, concat_axis=0, tiled=True)  24.1 us
    all_to_all x1, waiting for transfers between devices, per_device(): lax.all_to_all(windows.reshape(512, 2, HD), GRP + COL, split_axis=0, conc...  15.2 us
    all_to_all x1, waiting for transfers between devices, per_device(): lax.all_to_all(parts.reshape(32, 56, HD), ('z', 'yb', 'l'), split_axis=0,...  12.7 us
    all_to_all x1, starting transfers between devices, per_device(): lax.all_to_all(windows.reshape(512, 2, HD), GRP + COL, split_axis=0, conc...  11.3 us
    all_to_all x1, blocking collectives, per_device(): q = lax.all_to_all(q, ('yb', 'l'), split_axis=0, concat_axis=0, tiled=True)  9.03 us
    pallas_call x1, Pallas kernels, attend(): pl.pallas_call(attend_kernel, out_shape=jax.ShapeDtypeStruct((8, 4, 56, H...  8.3 us
    pallas_call x1, Pallas kernels, conv(): pl.pallas_call(conv_kernel, out_shape=jax.ShapeDtypeStruct((3, 16, PIX),...  6.62 us
  transfers between devices with their start and end apart: 5, of which 2 were waited for; matrix products, arithmetic and copies ran while one was open for 1% of the time, Pallas kernels for 5%

profile of v3, /device:TPU:1, one launch (start us, length us, event | category | flops | bytes accessed | tf_op | source)
XLA Modules:
  0.0 160.8 jit_solution(17931040793337872122)
XLA Ops:
  7.2 0.0 all-gather.3.cloned.1.call-start
  7.2 2.2 %shard_map.158 = (bf16[16,24,384]{2,1,0:T(8,128)(2,1)}, bf16[128,1536]{1,0:T(8,128)(2,1)}) custom-call(s32[1]{0:T(128)} %bitcast.1.c_ref, bf16[24,2048]{1,0:T(8,128)(2,1)} %bitcast.45, bf16[24,2048]{1,0:T(8,128)(2,1)} %bitcast.46, bf16[24,2048]{1,0:T(8,128)(2,1)} %bitcast.47, bf16[128,3072]{1,0:T(8,128)(2,1)} %weight_ref.1), custom_call_target="tpu_custom_call" | custom-call | tf_op jit(solution)/shard_map/pallas_call | solution.py:43
  9.4 0.0 all-gather.3.cloned.1.call-update
  9.5 24.1 %all_to_all.25 = bf16[16,24,384]{2,1,0:T(8,128)(2,1)S(1)} all-to-all(bf16[16,24,384]{2,1,0:T(8,128)(2,1)} %get-tuple-element.13), channel_id=1, replica_groups=mesh['h'=2,'z'=8,'ya'=4,'yb'=2,'l'=2,'c'=2] {'h','z'}, dimensions={0} | all-to-all | bytes 589824 | tf_op jit(solution)/shard_map/all_to_all | solution.py:386
  33.6 0.1 broadcast_in_dim.28
  33.6 27.1 %all_to_all.26 = bf16[4,384,256]{2,1,0:T(8,128)(2,1)S(1)} all-to-all(bf16[4,384,256]{2,1,0:T(8,128)(2,1)S(1)} %broadcast_in_dim.28), channel_id=1, replica_groups=mesh['h'=2,'z'=8,'ya'=4,'yb'=2,'l'=2,'c'=2] {'ya'}, dimensions={0} | all-to-all | bytes 1572864 | tf_op jit(solution)/shard_map/all_to_all | solution.py:389
  60.7 4.4 %collective-permute-start = (bf16[1536,256]{1,0:T(8,128)(2,1)S(1)}, bf16[1536,256]{1,0:T(8,128)(2,1)S(1)}, u32[]{:S(2)}, u32[]{:S(2)}) collective-permute-start(bf16[1536,256]{1,0:T(8,128)(2,1)S(1)} %bitcast.27), channel_id=1, source_target_pairs={{0,1},{1,0},{2,3},{3,2},{4,5},{5,4},{6,7},{7,6},{8,9},{9,8},{10,11... | collective-permute-start | bytes 2359304 | tf_op jit(solution)/shard_map/ppermute | solution.py:391
  65.1 0.1 broadcast_in_dim.27
  65.2 9.0 %all_to_all.27.q_ref = bf16[4,384,128]{2,1,0:T(8,128)(2,1)S(1)} all-to-all(bf16[4,384,128]{2,1,0:T(8,128)(2,1)S(1)} %broadcast_in_dim.27), channel_id=1, replica_groups=mesh['h'=2,'z'=8,'ya'=4,'yb'=2,'l'=2,'c'=2] {'yb','l'}, dimensions={0} | all-to-all | bytes 786432 | tf_op jit(solution)/shard_map/all_to_all | solution.py:393
  74.2 0.0 collective-permute-done.kv1_ref
  74.2 8.3 %shard_map.159 = bf16[8,4,56,128]{3,2,1,0:T(8,128)(2,1)} custom-call(bf16[4,384,128]{2,1,0:T(8,128)(2,1)S(1)} %all_to_all.27.q_ref, bf16[1536,256]{1,0:T(8,128)(2,1)S(1)} %bitcast.28, bf16[1536,256]{1,0:T(8,128)(2,1)S(1)} %collective-permute-done.kv1_ref), custom_call_target="tpu_custom_call" | custom-call | tf_op jit(solution)/shard_map/pallas_call | solution.py:111
  82.5 0.0 all-gather.3.cloned.1.call-done.own_ref
  82.5 3.3 %collective-permute-start.1 = (bf16[1024,1536]{1,0:T(8,128)(2,1)}, bf16[1024,1536]{1,0:T(8,128)(2,1)}, u32[]{:S(2)}, u32[]{:S(2)}) collective-permute-start(bf16[1024,1536]{1,0:T(8,128)(2,1)} %all-gather.3.cloned.1.call-done.own_ref), channel_id=1, source_target_pairs={{0,1},{1,0},{2,3},{3,2},{4,5},{5,4},{6,7},{7,6},{8,9},{9,8},{10,11... | collective-permute-start | bytes 9437192 | tf_op jit(solution)/shard_map/ppermute | solution.py:396
  85.8 5.6 %all-to-all-start.3 = ((bf16[32,56,128]{2,1,0:T(8,128)(2,1)}), bf16[32,56,128]{2,1,0:T(8,128)(2,1)}, u32[]{:S(2)}, u32[]{:S(2)}) async-start(bf16[32,56,128]{2,1,0:T(8,128)(2,1)} %bitcast.7), calls=%async_computation.3 | async-start | bytes 917504 | tf_op jit(solution)/shard_map/all_to_all | solution.py:398
  91.5 0.0 copy-start
  91.5 1.9 %copy-done = bf16[1024,1536]{1,0:T(8,128)(2,1)S(1)} copy-done((bf16[1024,1536]{1,0:T(8,128)(2,1)S(1)}, bf16[1024,1536]{1,0:T(8,128)(2,1)}, u32[]{:S(2)}) %copy-start) | copy-done | bytes 3145752
  93.3 0.2 shard_map.160.own_ref
  93.6 12.7 %all-to-all-done.3 = bf16[32,56,128]{2,1,0:T(8,128)(2,1)} async-done(((bf16[32,56,128]{2,1,0:T(8,128)(2,1)}), bf16[32,56,128]{2,1,0:T(8,128)(2,1)}, u32[]{:S(2)}, u32[]{:S(2)}) %all-to-all-start.3) | async-done | bytes 458784 | tf_op jit(solution)/shard_map/all_to_all | solution.py:398
  106.3 0.0 collective-permute-done.1.other_ref
  106.3 0.0 copy-start.2
  106.3 0.0 copy-start.3
  106.3 0.0 copy-start.4
  106.3 0.0 copy-start.5
  106.3 0.0 copy-start.6
  106.3 0.0 copy-start.7
  106.3 0.0 copy-start.9
  106.3 0.0 copy-start.10
  106.3 5.0 %shard_map.161 = (f32[24,3072]{1,0:T(8,128)S(1)}, bf16[24,3072]{1,0:T(8,128)(2,1)S(1)}) custom-call(s32[1]{0:T(128)} %bitcast.h_ref, s32[1]{0:T(128)} %bitcast.1.c_ref, bf16[8,4,56,128]{3,2,1,0:T(8,128)(2,1)} %bitcast.8.parts_ref, bf16[1024,1536]{1,0:T(8,128)(2,1)S(1)} %shard_map.160.own_ref, bf16[1024,1536]{1,0:T(8,128)(2,1)} %collective-permute-done.1.other_ref), custom_call_target="tpu_custom_call" | custom-call | tf_op jit(solution)/shard_map/pallas_call | solution.py:189
  111.3 0.0 copy-start.1
  111.4 0.0 copy-start.8
  111.4 6.3 %all-gather = bf16[48,3072]{1,0:T(8,128)(2,1)S(1)} all-gather(bf16[24,3072]{1,0:T(8,128)(2,1)S(1)} %get-tuple-element.18), channel_id=2, replica_groups=mesh['h'=2,'z'=8,'ya'=4,'yb'=2,'l'=2,'c'=2] {'h'}, dimensions={0}, use_global_device_ids=true | all-gather | bytes 442368 | tf_op jit(solution)/shard_map/all_gather | solution.py:402
  117.7 0.0 copy-done.2
  117.7 0.0 copy-done.3
  117.7 0.0 copy-done.4
  117.7 0.0 copy-done.5
  117.7 0.0 copy-done.6
  117.7 0.0 copy-done.7
  117.7 0.0 copy-done.9
  117.7 0.0 copy-done.10
  117.7 1.8 %shard_map.162 = (bf16[24,3072]{1,0:T(8,128)(2,1)}, bf16[16,32,2,128]{3,2,1,0:T(2,128)(2,1)}) custom-call(s32[1]{0:T(128)} %bitcast.h_ref, f32[24,3072]{1,0:T(8,128)S(1)} %get-tuple-element.17.keep_ref, bf16[2,24,3072]{2,1,0:T(8,128)(2,1)S(1)} %bitcast.30, bf16[24,3072]{1,0:T(8,128)(2,1)S(1)} %bitcast.34, bf16[2,24,3072]{2,1,0:T(8,128)(2,1)S(1)} %bitcast.33, ...), custom_call_target="tpu_custom_call" | custom-call | tf_op jit(solution)/shard_map/pallas_call | solution.py:254
  119.5 11.3 %all-to-all-start.4 = ((bf16[512,2,128]{2,1,0:T(2,128)(2,1)}), bf16[512,2,128]{2,1,0:T(2,128)(2,1)S(1)}, u32[]{:S(2)}, u32[]{:S(2)}) async-start(bf16[512,2,128]{2,1,0:T(2,128)(2,1)} %bitcast.21), calls=%async_computation.4 | async-start | bytes 524288 | tf_op jit(solution)/shard_map/all_to_all | solution.py:417
  130.8 1.0 copy.17
  131.9 0.0 copy-done.1
  131.9 0.2 shard_map.163.weights_ref
  132.1 15.2 %all-to-all-done.4.lat_ref = bf16[512,2,128]{2,1,0:T(2,128)(2,1)S(1)} async-done(((bf16[512,2,128]{2,1,0:T(2,128)(2,1)}), bf16[512,2,128]{2,1,0:T(2,128)(2,1)S(1)}, u32[]{:S(2)}, u32[]{:S(2)}) %all-to-all-start.4) | async-done | bytes 262176 | tf_op jit(solution)/shard_map/all_to_all | solution.py:417
  147.3 0.0 copy-done.8
  147.3 6.6 %shard_map.164 = bf16[3,16,1024]{2,1,0:T(8,128)(2,1)} custom-call(s32[1]{0:T(128)} %bitcast.19.band_ref, s32[1]{0:T(128)} %bitcast.20.own_ref, bf16[512,2,128]{2,1,0:T(2,128)(2,1)S(1)} %all-to-all-done.4.lat_ref, bf16[944,512]{1,0:T(8,128)(2,1)S(1)} %shard_map.163.weights_ref, f32[1,512]{1,0:T(1,128)S(1)} %bitcast.38), custom_call_target="tpu_custom_call" | custom-call | tf_op jit(solution)/shard_map/pallas_call | solution.py:348
  (2 shorter events, 0.0 us)
Async XLA Ops:
  7.2 75.3 %all-gather.3.cloned.1.call-start = ((), (), s32[]{:S(2)}) async-start(), calls=%async_computation.5 | async-start | bytes 3538944 | tf_op jit(solution)/shard_map/all_gather | solution.py:385
  60.7 13.5 %collective-permute-start = (bf16[1536,256]{1,0:T(8,128)(2,1)S(1)}, bf16[1536,256]{1,0:T(8,128)(2,1)S(1)}, u32[]{:S(2)}, u32[]{:S(2)}) collective-permute-start(bf16[1536,256]{1,0:T(8,128)(2,1)S(1)} %bitcast.27), channel_id=1, source_target_pairs={{0,1},{1,0},{2,3},{3,2},{4,5},{5,4},{6,7},{7,6},{8,9},{9,8},{10,11... | collective-permute-start | bytes 2359304 | tf_op jit(solution)/shard_map/ppermute | solution.py:391
  82.5 23.8 %collective-permute-start.1 = (bf16[1024,1536]{1,0:T(8,128)(2,1)}, bf16[1024,1536]{1,0:T(8,128)(2,1)}, u32[]{:S(2)}, u32[]{:S(2)}) collective-permute-start(bf16[1024,1536]{1,0:T(8,128)(2,1)} %all-gather.3.cloned.1.call-done.own_ref), channel_id=1, source_target_pairs={{0,1},{1,0},{2,3},{3,2},{4,5},{5,4},{6,7},{7,6},{8,9},{9,8},{10,11... | collective-permute-start | bytes 9437192 | tf_op jit(solution)/shard_map/ppermute | solution.py:396
  85.8 20.4 %all-to-all-start.3 = ((bf16[32,56,128]{2,1,0:T(8,128)(2,1)}), bf16[32,56,128]{2,1,0:T(8,128)(2,1)}, u32[]{:S(2)}, u32[]{:S(2)}) async-start(bf16[32,56,128]{2,1,0:T(8,128)(2,1)} %bitcast.7), calls=%async_computation.3 | async-start | bytes 917504 | tf_op jit(solution)/shard_map/all_to_all | solution.py:398
  91.5 1.9 %copy-start = (bf16[1024,1536]{1,0:T(8,128)(2,1)S(1)}, bf16[1024,1536]{1,0:T(8,128)(2,1)}, u32[]{:S(2)}) copy-start(bf16[1024,1536]{1,0:T(8,128)(2,1)} %all-gather.3.cloned.1.call-done.own_ref) | copy-start | bytes 9437188
  106.3 11.4 %copy-start.2 = (bf16[3072,64]{0,1:T(8,128)(2,1)S(1)}, bf16[3072,64]{0,1:T(8,128)(2,1)}, u32[]{:S(2)}) copy-start(bf16[3072,64]{0,1:T(8,128)(2,1)} %param.25) | copy-start | bytes 1179652
  106.3 11.4 %copy-start.3 = (bf16[2,1,1,24,3072]{4,3,2,1,0:T(8,128)(2,1)S(1)}, bf16[2,1,1,24,3072]{4,3,2,1,0:T(8,128)(2,1)}, u32[]{:S(2)}) copy-start(bf16[2,1,1,24,3072]{4,3,2,1,0:T(8,128)(2,1)} %param.16) | copy-start | bytes 884740
  106.3 11.4 %copy-start.4 = (bf16[1,1,24,3072]{3,2,1,0:T(8,128)(2,1)S(1)}, bf16[1,1,24,3072]{3,2,1,0:T(8,128)(2,1)}, u32[]{:S(2)}) copy-start(bf16[1,1,24,3072]{3,2,1,0:T(8,128)(2,1)} %param.15) | copy-start | bytes 442372
  106.3 11.4 %copy-start.5 = (f32[3072]{0:T(1024)S(1)}, f32[3072]{0:T(1024)}, u32[]{:S(2)}) copy-start(f32[3072]{0:T(1024)} %param.21) | copy-start | bytes 36868
  106.3 11.4 %copy-start.6 = (f32[3072]{0:T(1024)S(1)}, f32[3072]{0:T(1024)}, u32[]{:S(2)}) copy-start(f32[3072]{0:T(1024)} %param.22) | copy-start | bytes 36868
  106.3 11.4 %copy-start.7 = (f32[3072]{0:T(1024)S(1)}, f32[3072]{0:T(1024)}, u32[]{:S(2)}) copy-start(f32[3072]{0:T(1024)} %param.23) | copy-start | bytes 36868
  106.3 11.4 %copy-start.9 = (s32[2,1,1,24]{3,2,1,0:T(1,128)S(1)}, s32[2,1,1,24]{3,2,1,0:T(1,128)}, u32[]{:S(2)}) copy-start(s32[2,1,1,24]{3,2,1,0:T(1,128)} %param.17) | copy-start | bytes 580
  106.3 11.4 %copy-start.10 = (f32[64]{0:T(128)S(1)}, f32[64]{0:T(128)}, u32[]{:S(2)}) copy-start(f32[64]{0:T(128)} %param.26) | copy-start | bytes 772
  111.3 20.5 %copy-start.1 = (bf16[3,3,3,16,512]{4,3,2,1,0:T(8,128)(2,1)S(1)}, bf16[3,3,3,16,512]{4,3,2,1,0:T(8,128)(2,1)}, u32[]{:S(2)}) copy-start(bf16[3,3,3,16,512]{4,3,2,1,0:T(8,128)(2,1)} %param.27) | copy-start | bytes 1327108
  111.4 36.0 %copy-start.8 = (f32[512]{0:T(512)S(1)}, f32[512]{0:T(512)}, u32[]{:S(2)}) copy-start(f32[512]{0:T(512)} %param.28) | copy-start | bytes 6148
  119.5 27.8 %all-to-all-start.4 = ((bf16[512,2,128]{2,1,0:T(2,128)(2,1)}), bf16[512,2,128]{2,1,0:T(2,128)(2,1)S(1)}, u32[]{:S(2)}, u32[]{:S(2)}) async-start(bf16[512,2,128]{2,1,0:T(2,128)(2,1)} %bitcast.21), calls=%async_computation.4 | async-start | bytes 524288 | tf_op jit(solution)/shard_map/all_to_all | solution.py:417
Sparse Core Ops, SparseCore 0:
  10.1 53.7 all-gather.2

commit v4 on v3

--- a/solution.py
+++ b/solution.py
@@ -30,9 +30,8 @@
 
 
 def pack_kernel(c_ref, q_ref, k_ref, v_ref, weight_ref, out_ref, half_ref):
-    half = half_ref.shape[1]
-    half_ref[...] = weight_ref[:, pl.ds(pl.multiple_of(c_ref[0] * half, 128), half)]
-    for g in range(HEADS):
+    half_ref[...] = weight_ref[...]
+    for g in range(out_ref.shape[0]):
         cols = slice(g * HD, (g + 1) * HD)
         out_ref[g, :, 0:HD] = q_ref[:, cols]
         out_ref[g, :, HD : 2 * HD] = k_ref[:, cols]
@@ -40,14 +39,25 @@
 
 
 def pack(c, q, k, v, weight):
+    depth, width = weight.shape
+    steps = 2
+    tokens = pl.BlockSpec((TOK, HEADS * HD // steps), lambda i, c_ref: (0, i))
     return pl.pallas_call(
         pack_kernel,
         out_shape=(
             jax.ShapeDtypeStruct((HEADS, TOK, 3 * HD), BF16),
-            jax.ShapeDtypeStruct((weight.shape[0], weight.shape[1] // 2), BF16),
-        ),
-        in_specs=[SMEM] + [VMEM] * 4,
-        out_specs=(VMEM, VMEM),
+            jax.ShapeDtypeStruct((depth, width // 2), BF16),
+        ),
+        grid_spec=pltpu.PrefetchScalarGridSpec(
+            num_scalar_prefetch=1,
+            grid=(steps,),
+            in_specs=[tokens] * 3
+            + [pl.BlockSpec((depth // steps, width // 2), lambda i, c_ref: (i, c_ref[0]))],
+            out_specs=(
+                pl.BlockSpec((HEADS // steps, TOK, 3 * HD), lambda i, c_ref: (i, 0, 0)),
+                pl.BlockSpec((depth // steps, width // 2), lambda i, c_ref: (i, 0)),
+            ),
+        ),
     )(c, q, k, v, weight)
 
 
@@ -117,45 +127,51 @@
     )(q, *kvs)
 
 
-def hold_kernel(own_ref, out_ref, sem):
-    copy = pltpu.make_async_copy(own_ref, out_ref, sem)
-    copy.start()
-    copy.wait()
-
-
-def hold(own):
-    return pl.pallas_call(
-        hold_kernel,
-        out_shape=jax.ShapeDtypeStruct(own.shape, BF16),
-        in_specs=[pl.BlockSpec(memory_space=pltpu.HBM)],
-        out_specs=VMEM,
-        scratch_shapes=[pltpu.SemaphoreType.DMA],
-        cost_estimate=pl.CostEstimate(flops=0, bytes_accessed=2 * own.size * 2, transcendentals=0),
-        compiler_params=pltpu.CompilerParams(vmem_limit_bytes=8 * MIB),
-    )(own)
-
-
-def project_kernel(h_ref, c_ref, parts_ref, own_ref, other_ref, keep_ref, send_ref, att_ref, sum_ref):
+def project_kernel(
+    h_ref, c_ref, parts_ref, own_ref, other_ref, keep_ref, send_ref,
+    near_ref, far_ref, att_ref, sum_ref, part_sems, far_sems,
+):
     step = pl.program_id(0)
+    block = sum_ref.shape[1]
+
+    def far_copy(n):
+        return pltpu.make_async_copy(
+            other_ref.at[:, n * block : (n + 1) * block], far_ref.at[n], far_sems.at[n]
+        )
 
     @pl.when(step == 0)
     def join():
-        join_parts(parts_ref, att_ref)
+        copies = [
+            pltpu.make_async_copy(
+                parts_ref.at[pl.ds(n * 4, 4)], near_ref.at[pl.ds(n * 4, 4)], part_sems.at[n]
+            )
+            for n in range(2)
+        ]
+        for copy in copies:
+            copy.start()
+        for n in range(2):
+            far_copy(n).start()
+        for n, copy in enumerate(copies):
+            copy.wait()
+            join_parts(near_ref, att_ref, range(n * 4, n * 4 + 4))
 
     @pl.when(step < 2)
     def near():
         sum_ref[...] = dot(att_ref[...], own_ref[...], ((1,), (0,)))
 
-    @pl.when(step >= 2)
-    def far():
-        sum_ref[...] = dot(att_ref[...], other_ref[...], ((1,), (0,)))
+    for n in range(2):
+
+        @pl.when(step == 2 + n)
+        def far(n=n):
+            far_copy(n).wait()
+            sum_ref[...] = dot(att_ref[...], far_ref[n], ((1,), (0,)))
 
     h = h_ref[0]
     keep_ref[...] = sum_ref[pl.ds(pl.multiple_of(h * TOK, 8), TOK), :]
     send_ref[...] = sum_ref[pl.ds(pl.multiple_of((1 - h) * TOK, 8), TOK), :].astype(BF16)
 
 
-def join_parts(parts_ref, att_ref):
+def join_parts(parts_ref, att_ref, heads):
     token = lax.broadcasted_iota(jnp.int32, (2 * TOK, HD), 0)
     lane = lax.broadcasted_iota(jnp.int32, (2 * TOK, HD), 1)
     base = lane - lax.rem(token, 6) * 3
@@ -163,7 +179,7 @@
     spot = lax.broadcasted_iota(jnp.int32, (2 * TOK, 8), 0)
     row = lax.broadcasted_iota(jnp.int32, (2 * TOK, 8), 1)
     pick = jnp.where(lax.div(spot, 6) == row, 1.0, 0.0).astype(BF16)
-    for z in range(8):
+    for z in heads:
         logs = []
         pieces = [parts_ref[z, j].astype(F32) for j in range(4)]
         for j in range(4):
@@ -196,14 +212,18 @@
             num_scalar_prefetch=2,
             grid=(4,),
             in_specs=[
-                pl.BlockSpec(parts.shape, lambda i, h_ref, c_ref: (0, 0, 0, 0)),
+                pl.BlockSpec(memory_space=pl.ANY),
                 pl.BlockSpec((depth, block), lambda i, h_ref, c_ref: (0, jnp.minimum(i, 1))),
-                pl.BlockSpec((depth, block), lambda i, h_ref, c_ref: (0, jnp.maximum(i - 2, 0))),
+                pl.BlockSpec(memory_space=pl.ANY),
             ],
             out_specs=(pl.BlockSpec((TOK, block), place), pl.BlockSpec((TOK, block), place)),
             scratch_shapes=[
+                pltpu.VMEM(parts.shape, BF16),
+                pltpu.VMEM((2, depth, block), BF16),
                 pltpu.VMEM((2 * TOK, depth), BF16),
                 pltpu.VMEM((2 * TOK, block), F32),
+                pltpu.SemaphoreType.DMA((2,)),
+                pltpu.SemaphoreType.DMA((2,)),
             ],
         ),
         compiler_params=pltpu.CompilerParams(vmem_limit_bytes=24 * MIB),
@@ -394,7 +414,8 @@
     parts = attend(q, kvs)
     parts, mine = lax.optimization_barrier((parts, mine))
     theirs = lax.ppermute(mine, "c", [(0, 1), (1, 0)])
-    mine = hold(mine)
+    one = jnp.where(c[0] >= 0, 1.0, 0.0).astype(BF16)
+    mine = mine * one
     parts = lax.all_to_all(
         parts.reshape(32, 56, HD), ("z", "yb", "l"), split_axis=0, concat_axis=0, tiled=True
     )

time: 161 us -> 160 us (level)
  other arithmetic: 0 us -> 2.1 us
  local copies, waits for them, and re-layouts: 3.11 us -> 1.23 us
    mul x0 -> x1, other arithmetic: none -> 2.1 us  [per_device(): mine = mine * one]
    unnamed x22 -> x20, local copies, waits for them, and re-layouts: 1.94 us -> 0.06 us
  transfers between devices with their start and end apart: 5 -> 5, of which waited for: 2 -> 2; matrix products, arithmetic and copies ran while one was open for 1% -> 2% of each run, Pallas kernels for 5% -> 5%
where the time goes in v4:
time: 160 us
  blocking collectives  66.5 us (42%)
  waiting for transfers between devices  28.1 us (18%)
  starting transfers between devices  24.8 us (16%)
  Pallas kernels  22.9 us (14%)
  between operations  14.3 us (9%)
  other arithmetic  2.1 us (1%)
    all_to_all x1, blocking collectives, per_device(): kv = lax.all_to_all(kv, 'ya', split_axis=0, concat_axis=0, tiled=True)  27.1 us
    all_to_all x1, blocking collectives, per_device(): moved = lax.all_to_all(packed, GRP, split_axis=0, concat_axis=0, tiled=True)  24.1 us
    all_to_all x1, waiting for transfers between devices, per_device(): lax.all_to_all(windows.reshape(512, 2, HD), GRP + COL, split_axis=0, conc...  15.4 us
    all_to_all x1, waiting for transfers between devices, per_device(): lax.all_to_all(parts.reshape(32, 56, HD), ('z', 'yb', 'l'), split_axis=0,...  12.7 us
    all_to_all x1, starting transfers between devices, per_device(): lax.all_to_all(windows.reshape(512, 2, HD), GRP + COL, split_axis=0, conc...  11 us
    all_to_all x1, blocking collectives, per_device(): q = lax.all_to_all(q, ('yb', 'l'), split_axis=0, concat_axis=0, tiled=True)  9.03 us
    pallas_call x1, Pallas kernels, attend(): pl.pallas_call(attend_kernel, out_shape=jax.ShapeDtypeStruct((8, 4, 56, H...  8.29 us
    pallas_call x1, Pallas kernels, conv(): pl.pallas_call(conv_kernel, out_shape=jax.ShapeDtypeStruct((3, 16, PIX),...  6.62 us
  transfers between devices with their start and end apart: 5, of which 2 were waited for; matrix products, arithmetic and copies ran while one was open for 2% of the time, Pallas kernels for 5%

profile of v4, /device:TPU:1, one launch (start us, length us, event | category | flops | bytes accessed | tf_op | source)
XLA Modules:
  0.0 159.8 jit_solution(15019253891788999693)
XLA Ops:
  7.2 0.0 all-gather.3.cloned.1.call-start
  7.2 2.0 %shard_map.158 = (bf16[16,24,384]{2,1,0:T(8,128)(2,1)}, bf16[128,1536]{1,0:T(8,128)(2,1)}) custom-call(s32[1]{0:T(128)} %bitcast.1.c_ref, bf16[24,2048]{1,0:T(8,128)(2,1)} %bitcast.45, bf16[24,2048]{1,0:T(8,128)(2,1)} %bitcast.46, bf16[24,2048]{1,0:T(8,128)(2,1)} %bitcast.47, bf16[128,3072]{1,0:T(8,128)(2,1)} %weight_ref.1), custom_call_target="tpu_custom_call" | custom-call | tf_op jit(solution)/shard_map/pallas_call | solution.py:45
  9.2 0.0 all-gather.3.cloned.1.call-update
  9.2 24.1 %all_to_all.25 = bf16[16,24,384]{2,1,0:T(8,128)(2,1)S(1)} all-to-all(bf16[16,24,384]{2,1,0:T(8,128)(2,1)} %get-tuple-element.13), channel_id=1, replica_groups=mesh['h'=2,'z'=8,'ya'=4,'yb'=2,'l'=2,'c'=2] {'h','z'}, dimensions={0} | all-to-all | bytes 589824 | tf_op jit(solution)/shard_map/all_to_all | solution.py:406
  33.3 0.1 broadcast_in_dim.28
  33.4 27.1 %all_to_all.26 = bf16[4,384,256]{2,1,0:T(8,128)(2,1)S(1)} all-to-all(bf16[4,384,256]{2,1,0:T(8,128)(2,1)S(1)} %broadcast_in_dim.28), channel_id=1, replica_groups=mesh['h'=2,'z'=8,'ya'=4,'yb'=2,'l'=2,'c'=2] {'ya'}, dimensions={0} | all-to-all | bytes 1572864 | tf_op jit(solution)/shard_map/all_to_all | solution.py:409
  60.5 4.4 %collective-permute-start = (bf16[1536,256]{1,0:T(8,128)(2,1)S(1)}, bf16[1536,256]{1,0:T(8,128)(2,1)S(1)}, u32[]{:S(2)}, u32[]{:S(2)}) collective-permute-start(bf16[1536,256]{1,0:T(8,128)(2,1)S(1)} %bitcast.27), channel_id=1, source_target_pairs={{0,1},{1,0},{2,3},{3,2},{4,5},{5,4},{6,7},{7,6},{8,9},{9,8},{10,11... | collective-permute-start | bytes 2359304 | tf_op jit(solution)/shard_map/ppermute | solution.py:411
  64.9 0.1 broadcast_in_dim.27
  64.9 9.0 %all_to_all.27.q_ref = bf16[4,384,128]{2,1,0:T(8,128)(2,1)S(1)} all-to-all(bf16[4,384,128]{2,1,0:T(8,128)(2,1)S(1)} %broadcast_in_dim.27), channel_id=1, replica_groups=mesh['h'=2,'z'=8,'ya'=4,'yb'=2,'l'=2,'c'=2] {'yb','l'}, dimensions={0} | all-to-all | bytes 786432 | tf_op jit(solution)/shard_map/all_to_all | solution.py:413
  74.0 0.0 collective-permute-done.kv1_ref
  74.0 8.3 %shard_map.159 = bf16[8,4,56,128]{3,2,1,0:T(8,128)(2,1)} custom-call(bf16[4,384,128]{2,1,0:T(8,128)(2,1)S(1)} %all_to_all.27.q_ref, bf16[1536,256]{1,0:T(8,128)(2,1)S(1)} %bitcast.28, bf16[1536,256]{1,0:T(8,128)(2,1)S(1)} %collective-permute-done.kv1_ref), custom_call_target="tpu_custom_call" | custom-call | tf_op jit(solution)/shard_map/pallas_call | solution.py:121
  82.3 0.0 all-gather.3.cloned.1.call-done
  82.3 3.3 %collective-permute-start.1 = (bf16[1024,1536]{1,0:T(8,128)(2,1)}, bf16[1024,1536]{1,0:T(8,128)(2,1)}, u32[]{:S(2)}, u32[]{:S(2)}) collective-permute-start(bf16[1024,1536]{1,0:T(8,128)(2,1)} %all-gather.3.cloned.1.call-done), channel_id=1, source_target_pairs={{0,1},{1,0},{2,3},{3,2},{4,5},{5,4},{6,7},{7,6},{8,9},{9,8},{10,11... | collective-permute-start | bytes 9437192 | tf_op jit(solution)/shard_map/ppermute | solution.py:416
  85.6 6.0 %all-to-all-start.3 = ((bf16[32,56,128]{2,1,0:T(8,128)(2,1)}), bf16[32,56,128]{2,1,0:T(8,128)(2,1)}, u32[]{:S(2)}, u32[]{:S(2)}) async-start(bf16[32,56,128]{2,1,0:T(8,128)(2,1)} %bitcast.7), calls=%async_computation.3 | async-start | bytes 917504 | tf_op jit(solution)/shard_map/all_to_all | solution.py:419
  91.6 2.1 %broadcast_multiply_fusion.own_ref = bf16[1024,1536]{1,0:T(8,128)(2,1)S(1)} fusion(bf16[1024,1536]{1,0:T(8,128)(2,1)} %all-gather.3.cloned.1.call-done, bf16[]{:T(256)S(6)} %select_n.4), kind=kLoop, calls=%fused_computation | loop fusion | flops 1572864 | bytes 6291458 | tf_op jit(solution)/shard_map/mul | solution.py:418
  93.7 12.7 %all-to-all-done.3 = bf16[32,56,128]{2,1,0:T(8,128)(2,1)} async-done(((bf16[32,56,128]{2,1,0:T(8,128)(2,1)}), bf16[32,56,128]{2,1,0:T(8,128)(2,1)}, u32[]{:S(2)}, u32[]{:S(2)}) %all-to-all-start.3) | async-done | bytes 458784 | tf_op jit(solution)/shard_map/all_to_all | solution.py:419
  106.4 0.0 collective-permute-done.1.other_ref
  106.4 0.0 copy-start.1
  106.4 0.0 copy-start.2
  106.4 0.0 copy-start.3
  106.4 0.0 copy-start.4
  106.4 0.0 copy-start.5
  106.4 0.0 copy-start.6
  106.5 0.0 copy-start.8
  106.5 0.0 copy-start.9
  106.5 4.0 %shard_map.160 = (f32[24,3072]{1,0:T(8,128)S(1)}, bf16[24,3072]{1,0:T(8,128)(2,1)S(1)}) custom-call(s32[1]{0:T(128)} %bitcast.h_ref, s32[1]{0:T(128)} %bitcast.1.c_ref, bf16[8,4,56,128]{3,2,1,0:T(8,128)(2,1)} %bitcast.8.parts_ref, bf16[1024,1536]{1,0:T(8,128)(2,1)S(1)} %broadcast_multiply_fusion.own_ref, bf16[1024,1536]{1,0:T(8,128)(2,1)} %collective-permute-done.1.other_ref), custom_call_target="tpu_custom_call" | custom-call | tf_op jit(solution)/shard_map/pallas_call | solution.py:205
  110.4 0.0 copy-start
  110.5 0.0 copy-start.7
  110.5 6.3 %all-gather = bf16[48,3072]{1,0:T(8,128)(2,1)S(1)} all-gather(bf16[24,3072]{1,0:T(8,128)(2,1)S(1)} %get-tuple-element.18), channel_id=2, replica_groups=mesh['h'=2,'z'=8,'ya'=4,'yb'=2,'l'=2,'c'=2] {'h'}, dimensions={0}, use_global_device_ids=true | all-gather | bytes 442368 | tf_op jit(solution)/shard_map/all_gather | solution.py:423
  116.8 0.0 copy-done.1
  116.8 0.0 copy-done.2
  116.8 0.0 copy-done.3
  116.8 0.0 copy-done.4
  116.8 0.0 copy-done.5
  116.8 0.0 copy-done.6
  116.8 0.0 copy-done.8
  116.8 0.0 copy-done.9
  116.8 1.8 %shard_map.161 = (bf16[24,3072]{1,0:T(8,128)(2,1)}, bf16[16,32,2,128]{3,2,1,0:T(2,128)(2,1)}) custom-call(s32[1]{0:T(128)} %bitcast.h_ref, f32[24,3072]{1,0:T(8,128)S(1)} %get-tuple-element.17.keep_ref, bf16[2,24,3072]{2,1,0:T(8,128)(2,1)S(1)} %bitcast.30, bf16[24,3072]{1,0:T(8,128)(2,1)S(1)} %bitcast.34, bf16[2,24,3072]{2,1,0:T(8,128)(2,1)S(1)} %bitcast.33, ...), custom_call_target="tpu_custom_call" | custom-call | tf_op jit(solution)/shard_map/pallas_call | solution.py:274
  118.6 11.0 %all-to-all-start.4 = ((bf16[512,2,128]{2,1,0:T(2,128)(2,1)}), bf16[512,2,128]{2,1,0:T(2,128)(2,1)S(1)}, u32[]{:S(2)}, u32[]{:S(2)}) async-start(bf16[512,2,128]{2,1,0:T(2,128)(2,1)} %bitcast.21), calls=%async_computation.4 | async-start | bytes 524288 | tf_op jit(solution)/shard_map/all_to_all | solution.py:438
  129.7 1.0 copy.17
  130.7 0.0 copy-done
  130.8 0.2 shard_map.162.weights_ref
  131.0 15.4 %all-to-all-done.4.lat_ref = bf16[512,2,128]{2,1,0:T(2,128)(2,1)S(1)} async-done(((bf16[512,2,128]{2,1,0:T(2,128)(2,1)}), bf16[512,2,128]{2,1,0:T(2,128)(2,1)S(1)}, u32[]{:S(2)}, u32[]{:S(2)}) %all-to-all-start.4) | async-done | bytes 262176 | tf_op jit(solution)/shard_map/all_to_all | solution.py:438
  146.3 0.0 copy-done.7
  146.4 6.6 %shard_map.163 = bf16[3,16,1024]{2,1,0:T(8,128)(2,1)} custom-call(s32[1]{0:T(128)} %bitcast.19.band_ref, s32[1]{0:T(128)} %bitcast.20.own_ref, bf16[512,2,128]{2,1,0:T(2,128)(2,1)S(1)} %all-to-all-done.4.lat_ref, bf16[944,512]{1,0:T(8,128)(2,1)S(1)} %shard_map.162.weights_ref, f32[1,512]{1,0:T(1,128)S(1)} %bitcast.38), custom_call_target="tpu_custom_call" | custom-call | tf_op jit(solution)/shard_map/pallas_call | solution.py:368
  (2 shorter events, 0.0 us)
Async XLA Ops:
  7.2 75.1 %all-gather.3.cloned.1.call-start = ((), (), s32[]{:S(2)}) async-start(), calls=%async_computation.5 | async-start | bytes 3538944 | tf_op jit(solution)/shard_map/all_gather | solution.py:405
  60.5 13.5 %collective-permute-start = (bf16[1536,256]{1,0:T(8,128)(2,1)S(1)}, bf16[1536,256]{1,0:T(8,128)(2,1)S(1)}, u32[]{:S(2)}, u32[]{:S(2)}) collective-permute-start(bf16[1536,256]{1,0:T(8,128)(2,1)S(1)} %bitcast.27), channel_id=1, source_target_pairs={{0,1},{1,0},{2,3},{3,2},{4,5},{5,4},{6,7},{7,6},{8,9},{9,8},{10,11... | collective-permute-start | bytes 2359304 | tf_op jit(solution)/shard_map/ppermute | solution.py:411
  82.3 24.2 %collective-permute-start.1 = (bf16[1024,1536]{1,0:T(8,128)(2,1)}, bf16[1024,1536]{1,0:T(8,128)(2,1)}, u32[]{:S(2)}, u32[]{:S(2)}) collective-permute-start(bf16[1024,1536]{1,0:T(8,128)(2,1)} %all-gather.3.cloned.1.call-done), channel_id=1, source_target_pairs={{0,1},{1,0},{2,3},{3,2},{4,5},{5,4},{6,7},{7,6},{8,9},{9,8},{10,11... | collective-permute-start | bytes 9437192 | tf_op jit(solution)/shard_map/ppermute | solution.py:416
  85.6 20.8 %all-to-all-start.3 = ((bf16[32,56,128]{2,1,0:T(8,128)(2,1)}), bf16[32,56,128]{2,1,0:T(8,128)(2,1)}, u32[]{:S(2)}, u32[]{:S(2)}) async-start(bf16[32,56,128]{2,1,0:T(8,128)(2,1)} %bitcast.7), calls=%async_computation.3 | async-start | bytes 917504 | tf_op jit(solution)/shard_map/all_to_all | solution.py:419
  106.4 10.4 %copy-start.1 = (bf16[3072,64]{0,1:T(8,128)(2,1)S(1)}, bf16[3072,64]{0,1:T(8,128)(2,1)}, u32[]{:S(2)}) copy-start(bf16[3072,64]{0,1:T(8,128)(2,1)} %param.25) | copy-start | bytes 1179652
  106.4 10.4 %copy-start.2 = (bf16[2,1,1,24,3072]{4,3,2,1,0:T(8,128)(2,1)S(1)}, bf16[2,1,1,24,3072]{4,3,2,1,0:T(8,128)(2,1)}, u32[]{:S(2)}) copy-start(bf16[2,1,1,24,3072]{4,3,2,1,0:T(8,128)(2,1)} %param.16) | copy-start | bytes 884740
  106.4 10.4 %copy-start.3 = (bf16[1,1,24,3072]{3,2,1,0:T(8,128)(2,1)S(1)}, bf16[1,1,24,3072]{3,2,1,0:T(8,128)(2,1)}, u32[]{:S(2)}) copy-start(bf16[1,1,24,3072]{3,2,1,0:T(8,128)(2,1)} %param.15) | copy-start | bytes 442372
  106.4 10.4 %copy-start.4 = (f32[3072]{0:T(1024)S(1)}, f32[3072]{0:T(1024)}, u32[]{:S(2)}) copy-start(f32[3072]{0:T(1024)} %param.21) | copy-start | bytes 36868
  106.4 10.4 %copy-start.5 = (f32[3072]{0:T(1024)S(1)}, f32[3072]{0:T(1024)}, u32[]{:S(2)}) copy-start(f32[3072]{0:T(1024)} %param.22) | copy-start | bytes 36868
  106.4 10.4 %copy-start.6 = (f32[3072]{0:T(1024)S(1)}, f32[3072]{0:T(1024)}, u32[]{:S(2)}) copy-start(f32[3072]{0:T(1024)} %param.23) | copy-start | bytes 36868
  106.5 10.4 %copy-start.8 = (s32[2,1,1,24]{3,2,1,0:T(1,128)S(1)}, s32[2,1,1,24]{3,2,1,0:T(1,128)}, u32[]{:S(2)}) copy-start(s32[2,1,1,24]{3,2,1,0:T(1,128)} %param.17) | copy-start | bytes 580
  106.5 10.4 %copy-start.9 = (f32[64]{0:T(128)S(1)}, f32[64]{0:T(128)}, u32[]{:S(2)}) copy-start(f32[64]{0:T(128)} %param.26) | copy-start | bytes 772
  110.4 20.3 %copy-start = (bf16[3,3,3,16,512]{4,3,2,1,0:T(8,128)(2,1)S(1)}, bf16[3,3,3,16,512]{4,3,2,1,0:T(8,128)(2,1)}, u32[]{:S(2)}) copy-start(bf16[3,3,3,16,512]{4,3,2,1,0:T(8,128)(2,1)} %param.27) | copy-start | bytes 1327108
  110.5 35.9 %copy-start.7 = (f32[512]{0:T(512)S(1)}, f32[512]{0:T(512)}, u32[]{:S(2)}) copy-start(f32[512]{0:T(512)} %param.28) | copy-start | bytes 6148
  118.6 27.7 %all-to-all-start.4 = ((bf16[512,2,128]{2,1,0:T(2,128)(2,1)}), bf16[512,2,128]{2,1,0:T(2,128)(2,1)S(1)}, u32[]{:S(2)}, u32[]{:S(2)}) async-start(bf16[512,2,128]{2,1,0:T(2,128)(2,1)} %bitcast.21), calls=%async_computation.4 | async-start | bytes 524288 | tf_op jit(solution)/shard_map/all_to_all | solution.py:438
Sparse Core Ops, SparseCore 0:
  10.1 53.7 all-gather.2

commit v5 on v4

--- a/solution.py
+++ b/solution.py
@@ -114,7 +114,7 @@
             out_ref[z, i] = jnp.concatenate([o[0, z], o[1, z], stats], axis=0).astype(BF16)
         return carry
 
-    lax.fori_loop(0, 4, column, 0)
+    lax.fori_loop(0, 4, column, 0, unroll=2)
 
 
 def attend(q, kvs):
@@ -334,7 +334,6 @@
             for t in range(3):
                 at = r * 48 + b * 16
                 taps_ref[t, at : at + 16, :] = frames_back(moved, 2 - t, lane16).astype(BF16)
-    acc_ref[...] = jnp.zeros_like(acc_ref)
     for r in range(5):
         patches = jnp.concatenate([taps_ref[t, r * 48 : r * 48 + 144, :] for t in range(3)], axis=0)
         first = dot(weights_ref[432:, 0:432], patches, ((1,), (0,))) + bias
@@ -351,7 +350,10 @@
         for a in range(low, high + 1):
             for t in range(3):
                 at = ((a - low) * 3 + t) * 48
-                acc_ref[r - a, t] += z[at : at + 48]
+                if a == 0:
+                    acc_ref[r - a, t] = z[at : at + 48]
+                else:
+                    acc_ref[r - a, t] += z[at : at + 48]
     for o in range(3):
         own = pl.ds(pl.multiple_of(lanes * 16, 16), 16)
         total = first_ref[o, own, :].astype(F32)

time: 160 us -> 160 us (level)
  no operation moved by 1% of the time
where the time goes in v5:
time: 160 us
  blocking collectives  66.5 us (42%)
  waiting for transfers between devices  28.1 us (18%)
  starting transfers between devices  24.8 us (16%)
  Pallas kernels  22.6 us (14%)
  between operations  14.3 us (9%)
  other arithmetic  2.1 us (1%)
    all_to_all x1, blocking collectives, per_device(): kv = lax.all_to_all(kv, 'ya', split_axis=0, concat_axis=0, tiled=True)  27.1 us
    all_to_all x1, blocking collectives, per_device(): moved = lax.all_to_all(packed, GRP, split_axis=0, concat_axis=0, tiled=True)  24.1 us
    all_to_all x1, waiting for transfers between devices, per_device(): lax.all_to_all(windows.reshape(512, 2, HD), GRP + COL, split_axis=0, conc...  15.4 us
    all_to_all x1, waiting for transfers between devices, per_device(): lax.all_to_all(parts.reshape(32, 56, HD), ('z', 'yb', 'l'), split_axis=0,...  12.7 us
    all_to_all x1, starting transfers between devices, per_device(): lax.all_to_all(windows.reshape(512, 2, HD), GRP + COL, split_axis=0, conc...  11 us
    all_to_all x1, blocking collectives, per_device(): q = lax.all_to_all(q, ('yb', 'l'), split_axis=0, concat_axis=0, tiled=True)  9.03 us
    pallas_call x1, Pallas kernels, attend(): pl.pallas_call(attend_kernel, out_shape=jax.ShapeDtypeStruct((8, 4, 56, H...  8.03 us
    pallas_call x1, Pallas kernels, conv(): pl.pallas_call(conv_kernel, out_shape=jax.ShapeDtypeStruct((3, 16, PIX),...  6.62 us
  transfers between devices with their start and end apart: 5, of which 2 were waited for; matrix products, arithmetic and copies ran while one was open for 2% of the time, Pallas kernels for 5%

profile of v5, /device:TPU:1, one launch (start us, length us, event | category | flops | bytes accessed | tf_op | source)
XLA Modules:
  0.0 159.6 jit_solution(3669455738704438893)
XLA Ops:
  7.2 0.0 all-gather.3.cloned.1.call-start
  7.2 2.0 %shard_map.158 = (bf16[16,24,384]{2,1,0:T(8,128)(2,1)}, bf16[128,1536]{1,0:T(8,128)(2,1)}) custom-call(s32[1]{0:T(128)} %bitcast.1.c_ref, bf16[24,2048]{1,0:T(8,128)(2,1)} %bitcast.45, bf16[24,2048]{1,0:T(8,128)(2,1)} %bitcast.46, bf16[24,2048]{1,0:T(8,128)(2,1)} %bitcast.47, bf16[128,3072]{1,0:T(8,128)(2,1)} %weight_ref.1), custom_call_target="tpu_custom_call" | custom-call | tf_op jit(solution)/shard_map/pallas_call | solution.py:45
  9.2 0.0 all-gather.3.cloned.1.call-update
  9.2 24.1 %all_to_all.25 = bf16[16,24,384]{2,1,0:T(8,128)(2,1)S(1)} all-to-all(bf16[16,24,384]{2,1,0:T(8,128)(2,1)} %get-tuple-element.13), channel_id=1, replica_groups=mesh['h'=2,'z'=8,'ya'=4,'yb'=2,'l'=2,'c'=2] {'h','z'}, dimensions={0} | all-to-all | bytes 589824 | tf_op jit(solution)/shard_map/all_to_all | solution.py:408
  33.3 0.1 broadcast_in_dim.28
  33.4 27.1 %all_to_all.26 = bf16[4,384,256]{2,1,0:T(8,128)(2,1)S(1)} all-to-all(bf16[4,384,256]{2,1,0:T(8,128)(2,1)S(1)} %broadcast_in_dim.28), channel_id=1, replica_groups=mesh['h'=2,'z'=8,'ya'=4,'yb'=2,'l'=2,'c'=2] {'ya'}, dimensions={0} | all-to-all | bytes 1572864 | tf_op jit(solution)/shard_map/all_to_all | solution.py:411
  60.5 4.4 %collective-permute-start = (bf16[1536,256]{1,0:T(8,128)(2,1)S(1)}, bf16[1536,256]{1,0:T(8,128)(2,1)S(1)}, u32[]{:S(2)}, u32[]{:S(2)}) collective-permute-start(bf16[1536,256]{1,0:T(8,128)(2,1)S(1)} %bitcast.27), channel_id=1, source_target_pairs={{0,1},{1,0},{2,3},{3,2},{4,5},{5,4},{6,7},{7,6},{8,9},{9,8},{10,11... | collective-permute-start | bytes 2359304 | tf_op jit(solution)/shard_map/ppermute | solution.py:413
  64.9 0.1 broadcast_in_dim.27
  64.9 9.0 %all_to_all.27.q_ref = bf16[4,384,128]{2,1,0:T(8,128)(2,1)S(1)} all-to-all(bf16[4,384,128]{2,1,0:T(8,128)(2,1)S(1)} %broadcast_in_dim.27), channel_id=1, replica_groups=mesh['h'=2,'z'=8,'ya'=4,'yb'=2,'l'=2,'c'=2] {'yb','l'}, dimensions={0} | all-to-all | bytes 786432 | tf_op jit(solution)/shard_map/all_to_all | solution.py:415
  74.0 0.0 collective-permute-done.kv1_ref
  74.0 8.0 %shard_map.159 = bf16[8,4,56,128]{3,2,1,0:T(8,128)(2,1)} custom-call(bf16[4,384,128]{2,1,0:T(8,128)(2,1)S(1)} %all_to_all.27.q_ref, bf16[1536,256]{1,0:T(8,128)(2,1)S(1)} %bitcast.28, bf16[1536,256]{1,0:T(8,128)(2,1)S(1)} %collective-permute-done.kv1_ref), custom_call_target="tpu_custom_call" | custom-call | tf_op jit(solution)/shard_map/pallas_call | solution.py:121
  82.0 0.0 all-gather.3.cloned.1.call-done
  82.0 3.3 %collective-permute-start.1 = (bf16[1024,1536]{1,0:T(8,128)(2,1)}, bf16[1024,1536]{1,0:T(8,128)(2,1)}, u32[]{:S(2)}, u32[]{:S(2)}) collective-permute-start(bf16[1024,1536]{1,0:T(8,128)(2,1)} %all-gather.3.cloned.1.call-done), channel_id=1, source_target_pairs={{0,1},{1,0},{2,3},{3,2},{4,5},{5,4},{6,7},{7,6},{8,9},{9,8},{10,11... | collective-permute-start | bytes 9437192 | tf_op jit(solution)/shard_map/ppermute | solution.py:418
  85.3 6.0 %all-to-all-start.3 = ((bf16[32,56,128]{2,1,0:T(8,128)(2,1)}), bf16[32,56,128]{2,1,0:T(8,128)(2,1)}, u32[]{:S(2)}, u32[]{:S(2)}) async-start(bf16[32,56,128]{2,1,0:T(8,128)(2,1)} %bitcast.7), calls=%async_computation.3 | async-start | bytes 917504 | tf_op jit(solution)/shard_map/all_to_all | solution.py:421
  91.3 2.1 %broadcast_multiply_fusion.own_ref = bf16[1024,1536]{1,0:T(8,128)(2,1)S(1)} fusion(bf16[1024,1536]{1,0:T(8,128)(2,1)} %all-gather.3.cloned.1.call-done, bf16[]{:T(256)S(6)} %select_n.4), kind=kLoop, calls=%fused_computation | loop fusion | flops 1572864 | bytes 6291458 | tf_op jit(solution)/shard_map/mul | solution.py:420
  93.4 12.7 %all-to-all-done.3 = bf16[32,56,128]{2,1,0:T(8,128)(2,1)} async-done(((bf16[32,56,128]{2,1,0:T(8,128)(2,1)}), bf16[32,56,128]{2,1,0:T(8,128)(2,1)}, u32[]{:S(2)}, u32[]{:S(2)}) %all-to-all-start.3) | async-done | bytes 458784 | tf_op jit(solution)/shard_map/all_to_all | solution.py:421
  106.2 0.0 collective-permute-done.1.other_ref
  106.2 0.0 copy-start.1
  106.2 0.0 copy-start.2
  106.2 0.0 copy-start.3
  106.2 0.0 copy-start.4
  106.2 0.0 copy-start.5
  106.2 0.0 copy-start.6
  106.2 0.0 copy-start.8
  106.2 0.0 copy-start.9
  106.2 4.0 %shard_map.160 = (f32[24,3072]{1,0:T(8,128)S(1)}, bf16[24,3072]{1,0:T(8,128)(2,1)S(1)}) custom-call(s32[1]{0:T(128)} %bitcast.h_ref, s32[1]{0:T(128)} %bitcast.1.c_ref, bf16[8,4,56,128]{3,2,1,0:T(8,128)(2,1)} %bitcast.8.parts_ref, bf16[1024,1536]{1,0:T(8,128)(2,1)S(1)} %broadcast_multiply_fusion.own_ref, bf16[1024,1536]{1,0:T(8,128)(2,1)} %collective-permute-done.1.other_ref), custom_call_target="tpu_custom_call" | custom-call | tf_op jit(solution)/shard_map/pallas_call | solution.py:205
  110.2 0.0 copy-start
  110.2 0.0 copy-start.7
  110.2 6.3 %all-gather = bf16[48,3072]{1,0:T(8,128)(2,1)S(1)} all-gather(bf16[24,3072]{1,0:T(8,128)(2,1)S(1)} %get-tuple-element.18), channel_id=2, replica_groups=mesh['h'=2,'z'=8,'ya'=4,'yb'=2,'l'=2,'c'=2] {'h'}, dimensions={0}, use_global_device_ids=true | all-gather | bytes 442368 | tf_op jit(solution)/shard_map/all_gather | solution.py:425
  116.5 0.0 copy-done.1
  116.5 0.0 copy-done.2
  116.5 0.0 copy-done.3
  116.5 0.0 copy-done.4
  116.6 0.0 copy-done.5
  116.6 0.0 copy-done.6
  116.6 0.0 copy-done.8
  116.6 0.0 copy-done.9
  116.6 1.8 %shard_map.161 = (bf16[24,3072]{1,0:T(8,128)(2,1)}, bf16[16,32,2,128]{3,2,1,0:T(2,128)(2,1)}) custom-call(s32[1]{0:T(128)} %bitcast.h_ref, f32[24,3072]{1,0:T(8,128)S(1)} %get-tuple-element.17.keep_ref, bf16[2,24,3072]{2,1,0:T(8,128)(2,1)S(1)} %bitcast.30, bf16[24,3072]{1,0:T(8,128)(2,1)S(1)} %bitcast.34, bf16[2,24,3072]{2,1,0:T(8,128)(2,1)S(1)} %bitcast.33, ...), custom_call_target="tpu_custom_call" | custom-call | tf_op jit(solution)/shard_map/pallas_call | solution.py:274
  118.4 11.0 %all-to-all-start.4 = ((bf16[512,2,128]{2,1,0:T(2,128)(2,1)}), bf16[512,2,128]{2,1,0:T(2,128)(2,1)S(1)}, u32[]{:S(2)}, u32[]{:S(2)}) async-start(bf16[512,2,128]{2,1,0:T(2,128)(2,1)} %bitcast.21), calls=%async_computation.4 | async-start | bytes 524288 | tf_op jit(solution)/shard_map/all_to_all | solution.py:440
  129.5 1.0 copy.17
  130.5 0.0 copy-done
  130.5 0.2 shard_map.162.weights_ref
  130.7 15.4 %all-to-all-done.4.lat_ref = bf16[512,2,128]{2,1,0:T(2,128)(2,1)S(1)} async-done(((bf16[512,2,128]{2,1,0:T(2,128)(2,1)}), bf16[512,2,128]{2,1,0:T(2,128)(2,1)S(1)}, u32[]{:S(2)}, u32[]{:S(2)}) %all-to-all-start.4) | async-done | bytes 262176 | tf_op jit(solution)/shard_map/all_to_all | solution.py:440
  146.1 0.0 copy-done.7
  146.1 6.6 %shard_map.163 = bf16[3,16,1024]{2,1,0:T(8,128)(2,1)} custom-call(s32[1]{0:T(128)} %bitcast.19.band_ref, s32[1]{0:T(128)} %bitcast.20.own_ref, bf16[512,2,128]{2,1,0:T(2,128)(2,1)S(1)} %all-to-all-done.4.lat_ref, bf16[944,512]{1,0:T(8,128)(2,1)S(1)} %shard_map.162.weights_ref, f32[1,512]{1,0:T(1,128)S(1)} %bitcast.38), custom_call_target="tpu_custom_call" | custom-call | tf_op jit(solution)/shard_map/pallas_call | solution.py:370
  (2 shorter events, 0.0 us)
Async XLA Ops:
  7.2 74.8 %all-gather.3.cloned.1.call-start = ((), (), s32[]{:S(2)}) async-start(), calls=%async_computation.5 | async-start | bytes 3538944 | tf_op jit(solution)/shard_map/all_gather | solution.py:407
  60.5 13.5 %collective-permute-start = (bf16[1536,256]{1,0:T(8,128)(2,1)S(1)}, bf16[1536,256]{1,0:T(8,128)(2,1)S(1)}, u32[]{:S(2)}, u32[]{:S(2)}) collective-permute-start(bf16[1536,256]{1,0:T(8,128)(2,1)S(1)} %bitcast.27), channel_id=1, source_target_pairs={{0,1},{1,0},{2,3},{3,2},{4,5},{5,4},{6,7},{7,6},{8,9},{9,8},{10,11... | collective-permute-start | bytes 2359304 | tf_op jit(solution)/shard_map/ppermute | solution.py:413
  82.0 24.2 %collective-permute-start.1 = (bf16[1024,1536]{1,0:T(8,128)(2,1)}, bf16[1024,1536]{1,0:T(8,128)(2,1)}, u32[]{:S(2)}, u32[]{:S(2)}) collective-permute-start(bf16[1024,1536]{1,0:T(8,128)(2,1)} %all-gather.3.cloned.1.call-done), channel_id=1, source_target_pairs={{0,1},{1,0},{2,3},{3,2},{4,5},{5,4},{6,7},{7,6},{8,9},{9,8},{10,11... | collective-permute-start | bytes 9437192 | tf_op jit(solution)/shard_map/ppermute | solution.py:418
  85.3 20.8 %all-to-all-start.3 = ((bf16[32,56,128]{2,1,0:T(8,128)(2,1)}), bf16[32,56,128]{2,1,0:T(8,128)(2,1)}, u32[]{:S(2)}, u32[]{:S(2)}) async-start(bf16[32,56,128]{2,1,0:T(8,128)(2,1)} %bitcast.7), calls=%async_computation.3 | async-start | bytes 917504 | tf_op jit(solution)/shard_map/all_to_all | solution.py:421
  106.2 10.4 %copy-start.1 = (bf16[3072,64]{0,1:T(8,128)(2,1)S(1)}, bf16[3072,64]{0,1:T(8,128)(2,1)}, u32[]{:S(2)}) copy-start(bf16[3072,64]{0,1:T(8,128)(2,1)} %param.25) | copy-start | bytes 1179652
  106.2 10.4 %copy-start.2 = (bf16[2,1,1,24,3072]{4,3,2,1,0:T(8,128)(2,1)S(1)}, bf16[2,1,1,24,3072]{4,3,2,1,0:T(8,128)(2,1)}, u32[]{:S(2)}) copy-start(bf16[2,1,1,24,3072]{4,3,2,1,0:T(8,128)(2,1)} %param.16) | copy-start | bytes 884740
  106.2 10.4 %copy-start.3 = (bf16[1,1,24,3072]{3,2,1,0:T(8,128)(2,1)S(1)}, bf16[1,1,24,3072]{3,2,1,0:T(8,128)(2,1)}, u32[]{:S(2)}) copy-start(bf16[1,1,24,3072]{3,2,1,0:T(8,128)(2,1)} %param.15) | copy-start | bytes 442372
  106.2 10.4 %copy-start.4 = (f32[3072]{0:T(1024)S(1)}, f32[3072]{0:T(1024)}, u32[]{:S(2)}) copy-start(f32[3072]{0:T(1024)} %param.21) | copy-start | bytes 36868
  106.2 10.4 %copy-start.5 = (f32[3072]{0:T(1024)S(1)}, f32[3072]{0:T(1024)}, u32[]{:S(2)}) copy-start(f32[3072]{0:T(1024)} %param.22) | copy-start | bytes 36868
  106.2 10.4 %copy-start.6 = (f32[3072]{0:T(1024)S(1)}, f32[3072]{0:T(1024)}, u32[]{:S(2)}) copy-start(f32[3072]{0:T(1024)} %param.23) | copy-start | bytes 36868
  106.2 10.4 %copy-start.8 = (s32[2,1,1,24]{3,2,1,0:T(1,128)S(1)}, s32[2,1,1,24]{3,2,1,0:T(1,128)}, u32[]{:S(2)}) copy-start(s32[2,1,1,24]{3,2,1,0:T(1,128)} %param.17) | copy-start | bytes 580
  106.2 10.4 %copy-start.9 = (f32[64]{0:T(128)S(1)}, f32[64]{0:T(128)}, u32[]{:S(2)}) copy-start(f32[64]{0:T(128)} %param.26) | copy-start | bytes 772
  110.2 20.3 %copy-start = (bf16[3,3,3,16,512]{4,3,2,1,0:T(8,128)(2,1)S(1)}, bf16[3,3,3,16,512]{4,3,2,1,0:T(8,128)(2,1)}, u32[]{:S(2)}) copy-start(bf16[3,3,3,16,512]{4,3,2,1,0:T(8,128)(2,1)} %param.27) | copy-start | bytes 1327108
  110.2 35.9 %copy-start.7 = (f32[512]{0:T(512)S(1)}, f32[512]{0:T(512)}, u32[]{:S(2)}) copy-start(f32[512]{0:T(512)} %param.28) | copy-start | bytes 6148
  118.4 27.7 %all-to-all-start.4 = ((bf16[512,2,128]{2,1,0:T(2,128)(2,1)}), bf16[512,2,128]{2,1,0:T(2,128)(2,1)S(1)}, u32[]{:S(2)}, u32[]{:S(2)}) async-start(bf16[512,2,128]{2,1,0:T(2,128)(2,1)} %bitcast.21), calls=%async_computation.4 | async-start | bytes 524288 | tf_op jit(solution)/shard_map/all_to_all | solution.py:440
Sparse Core Ops, SparseCore 0:
  10.1 53.7 all-gather.2
